TPU v7x, 128 devices: a whole 4x4x4 slice. The times are simulated.
128 devices in a mesh: section: 8 (over x, core), expert: 16 (over z, y).
Axes of the slice: x: 4, y: 4, z: 4, core: 2. Of those that a mesh axis runs over, the one named last changes fastest.
Arguments:
- sent_acts: bfloat16 [8, 1024, 2048], P('section', 'expert'), may hold values from -6 to 6
- stash: bfloat16 [8, 1024, 2048], P('section', 'expert'), may hold values from -6 to 6
- cotangents: bfloat16 [8, 1024, 2048], P('section', 'expert'), may hold values from -6 to 6
- norm_gain: bfloat16 [8, 2048], P('section'), may hold values from 0.5 to 1.5
- w_gate: bfloat16 [8, 16, 2048, 768], P('section', 'expert'), may hold values from -0.125 to 0.125
- w_up: bfloat16 [8, 16, 2048, 768], P('section', 'expert'), may hold values from -0.125 to 0.125
- w_down: bfloat16 [8, 16, 768, 2048], P('section', 'expert'), may hold values from -0.21875 to 0.21875
- routes_next: int32 [8, 1024, 8], P('section', 'expert'), may hold values from 0 to 15, all different within a row; in each aligned block of 64 rows (0 to 63, 64 to 127, ..., all dimensions but the last counted through in order) at most 48 rows name the same one
- gates_next: bfloat16 [8, 1024, 8], P('section', 'expert'), may hold values from 0.049804688 to 0.5
- routes_prev: int32 [8, 1024, 8], P('section', 'expert'), may hold values from 0 to 15, all different within a row; in each aligned block of 64 rows (0 to 63, 64 to 127, ..., all dimensions but the last counted through in order) at most 48 rows name the same one
- gates_prev: bfloat16 [8, 1024, 8], P('section', 'expert'), may hold values from 0.049804688 to 0.5
Outputs:
- fwd_out: bfloat16 [8, 1024, 2048], P('section', 'expert')
- bwd_out: bfloat16 [8, 1024, 2048], P('section', 'expert')
- gate_grad: bfloat16 [8, 1024, 8], P('section', 'expert')
- grad_w_gate: bfloat16 [8, 16, 2048, 768], P('section', 'expert')
- grad_w_up: bfloat16 [8, 16, 2048, 768], P('section', 'expert')
- grad_w_down: bfloat16 [8, 16, 768, 2048], P('section', 'expert')
Inputs may be any that keep to these rules, and one draw needn't show every extreme that they name: `routes_next`: each row names 8 different experts. At most 48 of the 64 tokens of one device choose one expert, and in some device's tokens some expert is chosen by exactly 48. `routes_prev`: each row names 8 different experts. At most 48 of the 64 tokens of one device choose one expert, and in some device's tokens some expert is chosen by exactly 48.
All inputs are finite; a program needn't handle non-finite values.
Results may differ from a plain program's by a relative error of at most 0.008.
Values may be sent and summed in bfloat16 or wider, within the bound.
No kernel may reach another device: no remote copies, remote signals or barrier semaphores. Data moves between devices by JAX's collectives and lax.ppermute only.
A program may use at most 128 MiB of HBM per device.

v0:
```python
import jax
import jax.numpy as jnp
from jax import lax
from jax.sharding import PartitionSpec as P

CAP = 48
EPS = 1e-06
LANES = 128
BF16 = jnp.bfloat16
F32 = jnp.float32


def shifted(array, axis, by):
    count = lax.axis_size(axis)
    return lax.ppermute(array, axis, [(i, (i + by) % count) for i in range(count)])


def mm(a, b, dims):
    return lax.dot_general(a, b, (dims, ((), ())), preferred_element_type=F32)


def rms_norm(rows, gain):
    values = rows.astype(F32)
    scale = lax.rsqrt(jnp.mean(values * values, axis=-1, keepdims=True) + EPS)
    unit = values * scale
    return (unit * gain).astype(BF16), unit, scale


def tables(routes, gates, experts):
    tokens = routes.shape[0]
    hit = (routes[:, :, None] == jnp.arange(experts, dtype=jnp.int32)[None, None, :]).astype(F32)
    chosen = jnp.sum(hit, axis=1)
    gate = jnp.sum(hit * gates.astype(F32)[:, :, None], axis=1)
    row = lax.broadcasted_iota(jnp.int32, (tokens, tokens), 0)
    col = lax.broadcasted_iota(jnp.int32, (tokens, tokens), 1)
    upto = (col <= row).astype(BF16)
    rank = mm(upto, chosen.astype(BF16), ((1,), (0,))) * chosen
    return hit, rank, gate


def spread_columns(experts):
    owner = lax.broadcasted_iota(jnp.int32, (experts, experts, CAP), 1)
    mine = lax.broadcasted_iota(jnp.int32, (experts, experts, CAP), 0)
    return (owner == mine).astype(BF16).reshape(experts, experts * CAP)


def pick_matrix(rank, columns, experts):
    place = lax.broadcasted_iota(jnp.int32, (1, experts, CAP), 2).astype(F32).reshape(1, experts * CAP) + 1.0
    return mm(rank.astype(BF16), columns, ((1,), (0,))) == place


def per_device(
    sent_acts,
    stash,
    cotangents,
    norm_gain,
    w_gate,
    w_up,
    w_down,
    routes_next,
    gates_next,
    routes_prev,
    gates_prev,
):
    experts = lax.axis_size("expert") * w_gate.shape[1]
    me = lax.axis_index("expert")
    gain = norm_gain[0].astype(F32)
    wg, wu, wd = w_gate[0, 0], w_up[0, 0], w_down[0, 0]
    tokens, width = sent_acts.shape[1:]
    blocks = experts
    columns = spread_columns(experts)

    cot = shifted(cotangents, "section", -1)[0]
    arrived = shifted(sent_acts, "section", 1)[0]

    prev_rows, unit_prev, scale_prev = rms_norm(stash[0], gain)
    hit_prev, rank_prev, gate_prev = tables(routes_prev[0], gates_prev[0], experts)
    extra = jnp.pad(gate_prev.astype(BF16), ((0, 0), (0, LANES - experts)))
    bundle = jnp.concatenate([prev_rows, cot, extra], axis=1)
    gathered = lax.all_gather(bundle, "expert", axis=0, tiled=True)

    next_rows, _, _ = rms_norm(arrived, gain)
    _, rank_next, gate_next = tables(routes_next[0], gates_next[0], experts)
    pick_next = pick_matrix(rank_next, columns, experts)
    send = mm(pick_next.astype(BF16), next_rows, ((0,), (0,))).astype(BF16)
    recv = lax.all_to_all(
        send.reshape(experts, CAP, width), "expert", split_axis=0, concat_axis=0, tiled=True
    ).reshape(blocks * CAP, width)
    pre_gate = mm(recv, wg, ((1,), (0,)))
    pre_up = mm(recv, wu, ((1,), (0,)))
    hidden = (jax.nn.silu(pre_gate) * pre_up).astype(BF16)
    out = mm(hidden, wd, ((1,), (0,))).astype(BF16)
    back = lax.all_to_all(
        out.reshape(blocks, CAP, width), "expert", split_axis=0, concat_axis=0, tiled=True
    ).reshape(experts * CAP, width)
    blend = jnp.where(pick_next, mm(gate_next.astype(BF16), columns, ((1,), (0,))), 0.0).astype(BF16)
    fwd_out = (arrived.astype(F32) + mm(blend, back, ((1,), (0,)))).astype(BF16)

    rows = gathered[:, :width]
    cots = gathered[:, width : 2 * width]
    gates = gathered[:, 2 * width :].astype(F32)
    lane = lax.broadcasted_iota(jnp.int32, gates.shape, 1)
    gate = jnp.sum(jnp.where(lane == me, gates, 0.0), axis=1, keepdims=True)
    pre_gate = mm(rows, wg, ((1,), (0,)))
    pre_up = mm(rows, wu, ((1,), (0,)))
    plain = mm(cots, wd, ((1,), (1,)))
    sigma = jax.nn.sigmoid(pre_gate)
    active = pre_gate * sigma
    hidden = (active * pre_up).astype(BF16)
    d_hidden = plain * gate
    d_gate = (d_hidden * pre_up * sigma * (1.0 + pre_gate * (1.0 - sigma))).astype(BF16)
    d_up = (d_hidden * active).astype(BF16)
    gated = (hidden.astype(F32) * gate).astype(BF16)
    token_dots = jnp.sum(hidden.astype(F32) * plain, axis=1).astype(BF16)

    taken = (gate > 0.0).astype(F32).reshape(blocks, tokens)
    row = lax.broadcasted_iota(jnp.int32, (tokens, tokens), 0)
    col = lax.broadcasted_iota(jnp.int32, (tokens, tokens), 1)
    rank = mm(taken.astype(BF16), (row <= col).astype(BF16), ((1,), (0,))) * taken
    place = lax.broadcasted_iota(jnp.int32, (1, CAP, 1), 1).astype(F32) + 1.0
    pack = (rank[:, None, :] == place).astype(BF16)

    both = jnp.concatenate([d_gate, d_up], axis=1).reshape(blocks, tokens, -1)
    both = jnp.einsum("bct,btf->bcf", pack, both, preferred_element_type=F32).astype(BF16)
    both = both.reshape(blocks * CAP, -1)
    ff = wg.shape[1]
    row_grad = (
        mm(both[:, :ff], wg, ((1,), (1,))) + mm(both[:, ff:], wu, ((1,), (1,)))
    ).astype(BF16)
    grads = lax.all_to_all(
        row_grad.reshape(blocks, CAP, width), "expert", split_axis=0, concat_axis=0, tiled=True
    ).reshape(experts * CAP, width)
    dots = lax.all_gather(token_dots, "expert", axis=0, tiled=True).reshape(experts, blocks, tokens)

    grad_gate = mm(rows, d_gate, ((0,), (0,))).astype(BF16)
    grad_up = mm(rows, d_up, ((0,), (0,))).astype(BF16)
    grad_down = mm(gated, cots, ((0,), (0,))).astype(BF16)

    mine = lax.dynamic_index_in_dim(dots, me, axis=1, keepdims=False).astype(F32)
    gate_grad = jnp.sum(hit_prev * mine.T[:, None, :], axis=2).astype(BF16)

    pick_prev = pick_matrix(rank_prev, columns, experts).astype(BF16)
    summed = mm(pick_prev, grads, ((1,), (0,)))
    dxhat = summed * gain
    bwd_out = cot.astype(F32) + scale_prev * (
        dxhat - unit_prev * jnp.mean(dxhat * unit_prev, axis=-1, keepdims=True)
    )
    return (
        fwd_out[None],
        bwd_out.astype(BF16)[None],
        gate_grad[None],
        grad_gate[None, None],
        grad_up[None, None],
        grad_down[None, None],
    )


def solution(mesh):
    tokens = P("section", "expert", None)
    weight = P("section", "expert", None, None)
    return jax.shard_map(
        per_device,
        mesh=mesh,
        in_specs=(tokens, tokens, tokens, P("section", None), weight, weight, weight, tokens, tokens, tokens, tokens),
        out_specs=(tokens, tokens, tokens, weight, weight, weight),
        check_vma=False,
    )
```

profile of v0, /device:TPU:0, one launch (start us, length us, event | category | flops | bytes accessed | tf_op | source)
XLA Modules:
  0.0 289.0 jit_solution(14580354235956374943)
XLA Ops:
  7.2 2.3 collective-permute-start.1
  9.5 1.1 fusion.56
  11.3 0.7 mul.180
  12.0 0.7 select_reduce_fusion.2
  12.8 1.1 fusion.50
  13.9 1.8 fusion.49
  16.5 0.7 select_reduce_fusion.3
  17.7 5.3 %collective-permute-done = bf16[1,64,2048]{2,1,0:T(8,128)(2,1)S(1)} collective-permute-done((bf16[1,64,2048]{2,1,0:T(8,128)(2,1)}, bf16[1,64,2048]{2,1,0:T(8,128)(2,1)S(1)}, u32[]{:S(2)}, u32[]{:S(2)}) %collective-permute-start) | collective-permute-done | bytes 262176 | tf_op jit(solution)/shard_map/ppermute | solution.py:15
  23.1 2.7 convolution_convert_fusion.4
  25.9 8.1 %all-to-all-start = ((bf16[16,48,2048]{2,1,0:T(8,128)(2,1)}), bf16[16,48,2048]{2,1,0:T(8,128)(2,1)}, u32[]{:S(2)}, u32[]{:S(2)}) async-start(bf16[16,48,2048]{2,1,0:T(8,128)(2,1)} %bitcast.84), calls=%async_computation | async-start | bytes 6291456 | tf_op jit(solution)/shard_map/all_to_all | solution.py:86
  34.0 49.7 %all-to-all-done = bf16[16,48,2048]{2,1,0:T(8,128)(2,1)} async-done(((bf16[16,48,2048]{2,1,0:T(8,128)(2,1)}), bf16[16,48,2048]{2,1,0:T(8,128)(2,1)}, u32[]{:S(2)}, u32[]{:S(2)}) %all-to-all-start) | async-done | bytes 3145760 | tf_op jit(solution)/shard_map/all_to_all | solution.py:86
  83.7 6.9 %fusion.14 = f32[768,768]{1,0:T(8,128)} fusion(bf16[768,2048]{1,0:T(8,128)(2,1)} %bitcast.6, bf16[1,1,2048,768]{3,2,1,0:T(8,128)(2,1)} %param.16), kind=kOutput, calls=%fused_computation.21 | convolution fusion | flops 2415919104 | bytes 8650752 | tf_op jit(solution)/shard_map/dot_general | solution.py:19
  90.5 11.1 %convolution_convert_fusion.3 = bf16[768,2048]{1,0:T(8,128)(2,1)} fusion(bf16[1,1,768,2048]{3,2,1,0:T(8,128)(2,1)S(1)} %copy-done, f32[768,768]{1,0:T(8,128)} %fusion.14, bf16[768,2048]{1,0:T(8,128)(2,1)} %bitcast.6, bf16[1,1,2048,768]{3,2,1,0:T(8,128)(2,1)} %param.15), kind=kOutput, calls=%fused_computation.11 | convolution fusion | flops 4836950016 | bytes 14942208 | tf_op jit(solution)/shard_map/dot_general | solution.py:19
  101.7 4.7 %all-to-all-start.1 = ((bf16[16,48,2048]{2,1,0:T(8,128)(2,1)}), bf16[16,48,2048]{2,1,0:T(8,128)(2,1)}, u32[]{:S(2)}, u32[]{:S(2)}) async-start(bf16[16,48,2048]{2,1,0:T(8,128)(2,1)} %bitcast.86), calls=%async_computation.1 | async-start | bytes 6291456 | tf_op jit(solution)/shard_map/all_to_all | solution.py:93
  106.3 47.0 %all-gather.2.cloned.1.call-done = bf16[1024,4224]{1,0:T(8,128)(2,1)} async-done(((bf16[64,4224]{1,0:T(8,128)(2,1)}), bf16[1024,4224]{1,0:T(8,128)(2,1)}) %all-gather.2.cloned.1.call-update) | async-done | bytes 8650768 | tf_op jit(solution)/shard_map/all_gather | solution.py:80
  153.4 6.4 %fusion.18 = f32[1024,768]{0,1:T(8,128)S(1)} fusion(bf16[1,1,2048,768]{3,2,1,0:T(8,128)(2,1)} %param.15, bf16[1024,4224]{1,0:T(8,128)(2,1)} %all-gather.2.cloned.1.call-done), kind=kOutput, calls=%fused_computation.25 | convolution fusion | flops 3221225472 | bytes 10485760 | tf_op jit(solution)/shard_map/dot_general | solution.py:19
  159.9 3.6 %fusion.12 = f32[1024,768]{0,1:T(8,128)S(1)} fusion(bf16[1,1,2048,768]{3,2,1,0:T(8,128)(2,1)S(1)} %copy-done.8, bf16[1024,4224]{1,0:T(8,128)(2,1)S(1)} %copy-done.6), kind=kOutput, calls=%fused_computation.19 | convolution fusion | flops 3221225472 | bytes 10485760 | tf_op jit(solution)/shard_map/dot_general | solution.py:19
  163.7 6.6 %fusion.7 = (bf16[1024]{0:T(1024)(128)(2,1)S(1)}, bf16[1024,768]{0,1:T(8,128)(2,1)}, bf16[1024,768]{0,1:T(8,128)(2,1)}, bf16[1024,768]{0,1:T(8,128)(2,1)}) fusion(f32[1024,768]{0,1:T(8,128)S(1)} %fusion.12, f32[1024,768]{0,1:T(8,128)S(1)} %fusion.18, f32[1024]{0:T(1024)S(1)} %select_reduce_fusion, bf16[1,1,768,2048]{3,2,1,0:T(8,128)(2,1)S(1)} %copy-done, ...), kind=kOutput, calls=%fused_computation.13 | convolution fusion | flops 3236166656 | bytes 18356224 | tf_op jit(solution)/shard_map/dot_general | solution.py:19
  170.4 3.9 %pad_maximum_fusion = bf16[1024,1536]{0,1:T(8,128)(2,1)} fusion(bf16[1024,768]{0,1:T(8,128)(2,1)} %get-tuple-element.13, bf16[1024,768]{0,1:T(8,128)(2,1)} %get-tuple-element.12), kind=kLoop, calls=%fused_computation.15 | loop fusion | flops 6291456 | bytes 6291456 | tf_op jit(solution)/shard_map/concatenate | solution.py:123
  174.2 3.2 %copy.37 = bf16[1024,1536]{1,0:T(8,128)(2,1)S(1)} copy(bf16[1024,1536]{0,1:T(8,128)(2,1)} %pad_maximum_fusion) | data formatting | bytes 6291456 | tf_op jit(solution)/shard_map/concatenate | solution.py:123
  177.5 0.8 convolution_convert_fusion.2
  178.4 0.9 copy-done.7
  179.3 2.6 fusion.16
  181.9 4.1 %add_convert_fusion = bf16[768,2048]{1,0:T(8,128)(2,1)} fusion(f32[768,2048]{1,0:T(8,128)S(1)} %fusion.16, bf16[1,1,2048,768]{3,2,1,0:T(8,128)(2,1)S(1)} %copy-done.9, bf16[768,1536]{1,0:T(8,128)(2,1)S(1)} %bitcast.88), kind=kOutput, calls=%fused_computation | convolution fusion | flops 2419064832 | bytes 13762560 | tf_op jit(solution)/shard_map/dot_general | solution.py:19
  186.0 6.1 %all-to-all-start.2 = ((bf16[16,48,2048]{2,1,0:T(8,128)(2,1)}), bf16[16,48,2048]{2,1,0:T(8,128)(2,1)}, u32[]{:S(2)}, u32[]{:S(2)}) async-start(bf16[16,48,2048]{2,1,0:T(8,128)(2,1)} %bitcast.20), calls=%async_computation.2 | async-start | bytes 6291456 | tf_op jit(solution)/shard_map/all_to_all | solution.py:130
  192.1 3.5 %fusion.33 = bf16[1,64,2048]{2,1,0:T(8,128)(2,1)} fusion(bf16[768,2048]{1,0:T(8,128)(2,1)} %bitcast.11, pred[64,768]{1,0:T(32,128)(4,1)S(1)} %convolution_compare_fusion.1, bf16[1,64,2048]{2,1,0:T(8,128)(2,1)S(1)} %collective-permute-done, s32[768]{0:T(1024)S(1)} %iota.91, bf16[64,16]{0,1:T(8,128)(2,1)S(1)} %get-tuple-element.8), kind=kOutput, calls=%fused_computation.45 | convolution fusion | flops 203403264 | bytes 3724288 | tf_op jit(solution)/shard_map/dot_general | solution.py:19
  195.6 57.8 %all_gather.7 = bf16[16384]{0:T(1024)(128)(2,1)S(1)} all-gather(bf16[1024]{0:T(1024)(128)(2,1)S(1)} %get-tuple-element.10), channel_id=1, replica_groups=mesh['section'=8,'expert'=16] {'expert'}, dimensions={0}, use_global_device_ids=true | all-gather | bytes 34816 | tf_op jit(solution)/shard_map/all_gather | solution.py:133
  254.2 7.6 %fusion.23 = bf16[1,1,2048,768]{3,2,1,0:T(8,128)(2,1)} fusion(bf16[1024,768]{0,1:T(8,128)(2,1)S(1)} %copy-done.4, bf16[1024,4224]{1,0:T(8,128)(2,1)} %all-gather.2.cloned.1.call-done), kind=kOutput, calls=%fused_computation.34 | convolution fusion | flops 3222798336 | bytes 8912896 | tf_op jit(solution)/shard_map/dot_general | solution.py:19
  261.8 7.6 %fusion.24 = bf16[1,1,2048,768]{3,2,1,0:T(8,128)(2,1)} fusion(bf16[1024,768]{0,1:T(8,128)(2,1)S(1)} %copy-done.3, bf16[1024,4224]{1,0:T(8,128)(2,1)} %all-gather.2.cloned.1.call-done), kind=kOutput, calls=%fused_computation.35 | convolution fusion | flops 3222798336 | bytes 8912896 | tf_op jit(solution)/shard_map/dot_general | solution.py:19
  269.4 7.1 %fusion.25 = bf16[1,1,768,2048]{3,2,1,0:T(8,128)(2,1)} fusion(bf16[1024,4224]{1,0:T(8,128)(2,1)} %all-gather.2.cloned.1.call-done, bf16[1024,768]{0,1:T(8,128)(2,1)S(1)} %copy-done.10, f32[1024]{0:T(1024)S(1)} %select_reduce_fusion), kind=kOutput, calls=%fused_computation.36 | convolution fusion | flops 3225157632 | bytes 8916992 | tf_op jit(solution)/shard_map/dot_general | solution.py:19
  276.5 3.6 %fusion.51 = (f32[64]{0:T(128)S(1)}, f32[64,2048]{1,0:T(8,128)}) fusion(bf16[1,64,2048]{2,1,0:T(8,128)(2,1)S(1)} %copy-done.2, f32[64]{0:T(128)S(1)} %add_rsqrt_fusion, f32[2048]{0:T(1024)S(1)} %bitcast.91, bf16[768,2048]{1,0:T(8,128)(2,1)} %bitcast.21, bf16[64,16]{0,1:T(8,128)(2,1)S(1)} %fusion.42, f32[768]{0:T(1024)S(1)} %add.68, s32[768]{0:T(1024)S(1)} %iota.91), kind=kOutput, calls=%fused_computation.69 | convolution fusion | flops 203616192 | bytes 3949056 | tf_op jit(solution)/shard_map/dot_general | solution.py:19
  280.1 2.0 fusion.62
  (49 shorter events, 3.6 us)
Async XLA Ops:
  7.2 83.4 %copy-start = (bf16[1,1,768,2048]{3,2,1,0:T(8,128)(2,1)S(1)}, bf16[1,1,768,2048]{3,2,1,0:T(8,128)(2,1)}, u32[]{:S(2)}) copy-start(bf16[1,1,768,2048]{3,2,1,0:T(8,128)(2,1)} %param.17) | copy-start | bytes 9437188
  7.2 146.2 %all-gather.2.cloned.1.call-start = ((), (), s32[]{:S(2)}) async-start(), calls=%async_computation.3 | async-start | bytes 9191424 | tf_op jit(solution)/shard_map/all_gather | solution.py:80
  7.2 6.7 %collective-permute-start.1 = (bf16[1,64,2048]{2,1,0:T(8,128)(2,1)}, bf16[1,64,2048]{2,1,0:T(8,128)(2,1)}, u32[]{:S(2)}, u32[]{:S(2)}) collective-permute-start(bf16[1,64,2048]{2,1,0:T(8,128)(2,1)} %param.13), channel_id=1, source_target_pairs={{0,112},{16,0},{32,16},{48,32},{64,48},{80,64},{96,80},{112,96},{1... | collective-permute-start | bytes 786440 | tf_op jit(solution)/shard_map/ppermute | solution.py:15
  15.8 7.2 %collective-permute-start = (bf16[1,64,2048]{2,1,0:T(8,128)(2,1)}, bf16[1,64,2048]{2,1,0:T(8,128)(2,1)S(1)}, u32[]{:S(2)}, u32[]{:S(2)}) collective-permute-start(bf16[1,64,2048]{2,1,0:T(8,128)(2,1)} %param.11), channel_id=1, source_target_pairs={{0,16},{16,32},{32,48},{48,64},{64,80},{80,96},{96,112},{112,0},{1... | collective-permute-start | bytes 786440 | tf_op jit(solution)/shard_map/ppermute | solution.py:15
  25.9 57.8 %all-to-all-start = ((bf16[16,48,2048]{2,1,0:T(8,128)(2,1)}), bf16[16,48,2048]{2,1,0:T(8,128)(2,1)}, u32[]{:S(2)}, u32[]{:S(2)}) async-start(bf16[16,48,2048]{2,1,0:T(8,128)(2,1)} %bitcast.84), calls=%async_computation | async-start | bytes 6291456 | tf_op jit(solution)/shard_map/all_to_all | solution.py:86
  101.7 84.3 %all-to-all-start.1 = ((bf16[16,48,2048]{2,1,0:T(8,128)(2,1)}), bf16[16,48,2048]{2,1,0:T(8,128)(2,1)}, u32[]{:S(2)}, u32[]{:S(2)}) async-start(bf16[16,48,2048]{2,1,0:T(8,128)(2,1)} %bitcast.86), calls=%async_computation.1 | async-start | bytes 6291456 | tf_op jit(solution)/shard_map/all_to_all | solution.py:93
  153.4 6.4 %copy-start.6 = (bf16[1024,4224]{1,0:T(8,128)(2,1)S(1)}, bf16[1024,4224]{1,0:T(8,128)(2,1)}, u32[]{:S(2)}) copy-start(bf16[1024,4224]{1,0:T(8,128)(2,1)} %all-gather.2.cloned.1.call-done) | copy-start | bytes 25952260
  153.4 6.5 %copy-start.8 = (bf16[1,1,2048,768]{3,2,1,0:T(8,128)(2,1)S(1)}, bf16[1,1,2048,768]{3,2,1,0:T(8,128)(2,1)}, u32[]{:S(2)}) copy-start(bf16[1,1,2048,768]{3,2,1,0:T(8,128)(2,1)} %param.16) | copy-start | bytes 9437188
  177.4 1.9 copy-start.7
  179.3 2.6 copy-start.9
  186.0 90.5 %all-to-all-start.2 = ((bf16[16,48,2048]{2,1,0:T(8,128)(2,1)}), bf16[16,48,2048]{2,1,0:T(8,128)(2,1)}, u32[]{:S(2)}, u32[]{:S(2)}) async-start(bf16[16,48,2048]{2,1,0:T(8,128)(2,1)} %bitcast.20), calls=%async_computation.2 | async-start | bytes 6291456 | tf_op jit(solution)/shard_map/all_to_all | solution.py:130
  192.1 61.4 %copy-start.5 = (s32[1,64,8]{1,2,0:T(8,128)S(1)}, s32[1,64,8]{1,2,0:T(8,128)}, u32[]{:S(2)}) copy-start(s32[1,64,8]{1,2,0:T(8,128)} %param.20) | copy-start | bytes 6148
  192.1 62.2 %copy-start.4 = (bf16[1024,768]{0,1:T(8,128)(2,1)S(1)}, bf16[1024,768]{0,1:T(8,128)(2,1)}, u32[]{:S(2)}) copy-start(bf16[1024,768]{0,1:T(8,128)(2,1)} %get-tuple-element.12) | copy-start | bytes 4718596
  254.2 7.6 %copy-start.3 = (bf16[1024,768]{0,1:T(8,128)(2,1)S(1)}, bf16[1024,768]{0,1:T(8,128)(2,1)}, u32[]{:S(2)}) copy-start(bf16[1024,768]{0,1:T(8,128)(2,1)} %get-tuple-element.13) | copy-start | bytes 4718596
  261.8 7.6 %copy-start.10 = (bf16[1024,768]{0,1:T(8,128)(2,1)S(1)}, bf16[1024,768]{0,1:T(8,128)(2,1)}, u32[]{:S(2)}) copy-start(bf16[1024,768]{0,1:T(8,128)(2,1)} %get-tuple-element.11) | copy-start | bytes 4718596
  269.4 7.1 %copy-start.2 = (bf16[1,64,2048]{2,1,0:T(8,128)(2,1)S(1)}, bf16[1,64,2048]{2,1,0:T(8,128)(2,1)}, u32[]{:S(2)}) copy-start(bf16[1,64,2048]{2,1,0:T(8,128)(2,1)} %param.12) | copy-start | bytes 786436
  269.4 12.7 %copy-start.1 = (bf16[1,1,768,2048]{3,2,1,0:T(8,128)(2,1)S(1)}, bf16[1,1,768,2048]{3,2,1,0:T(8,128)(2,1)}, u32[]{:S(2)}) copy-start(bf16[1,1,768,2048]{3,2,1,0:T(8,128)(2,1)} %param.17) | copy-start | bytes 9437188
Sparse Core Ops, SparseCore 0:
  15.9 137.4 all-gather.1
where the time goes:
time: 290 us; the launch traced here: 289 us
  waiting for transfers between devices  102 us (35%)
  matrix products  74.8 us (26%)
  blocking collectives  57.8 us (20%)
  starting transfers between devices  21.2 us (7%)
  other arithmetic  14.3 us (5%)
  between operations  14.3 us (5%)
  local copies, waits for them, and re-layouts  4.71 us (2%)
    dot_general x16, matrix products, mm(): return lax.dot_general(a, b, (dims, ((), ())), preferred_element_type=F32)  74 us
    all_gather x1, blocking collectives, per_device(): lax.all_gather(token_dots, 'expert', axis=0, tiled=True)  57.8 us
    all_to_all x1, waiting for transfers between devices, per_device(): lax.all_to_all(send.reshape(experts, CAP, width), 'expert', split_axis=0,...  49.7 us
    all_gather x1, waiting for transfers between devices, per_device(): gathered = lax.all_gather(bundle, 'expert', axis=0, tiled=True)  47 us
    all_to_all x1, starting transfers between devices, per_device(): lax.all_to_all(send.reshape(experts, CAP, width), 'expert', split_axis=0,...  8.09 us
    all_to_all x1, starting transfers between devices, per_device(): lax.all_to_all(row_grad.reshape(blocks, CAP, width), 'expert', split_axis...  6.05 us
  transfers between devices with their start and end apart: 6, of which 3 were waited for; matrix products, arithmetic and copies ran while one was open for 30% of the time, Pallas kernels for 0%

commit v1 on v0

v1 whole, which is shorter than its diff:
```python
import functools
import math

import jax
import jax.numpy as jnp
from jax import lax
from jax.experimental import pallas as pl
from jax.experimental.pallas import tpu as pltpu
from jax.sharding import PartitionSpec as P

CAP = 48
EPS = 1e-06
LANES = 128
BF16 = jnp.bfloat16
F32 = jnp.float32
NN = ((1,), (0,))
NT = ((1,), (1,))
TN = ((0,), (0,))
SIDE = 4
GRANT = 48 * 1024 * 1024


def shifted(array, axis, by):
    count = lax.axis_size(axis)
    return lax.ppermute(array, axis, [(i, (i + by) % count) for i in range(count)])


def pull(array, along, d):
    if d % SIDE == 0:
        return array
    pairs = []
    for i in range(SIDE * SIDE):
        z, y = divmod(i, SIDE)
        source = ((z + d) % SIDE) * SIDE + y if along == "z" else z * SIDE + (y + d) % SIDE
        pairs.append((source, i))
    return lax.ppermute(array, "expert", pairs)


def mm(a, b, dims=NN):
    return lax.dot_general(a, b, (dims, ((), ())), preferred_element_type=F32)


def rms_norm(rows, gain):
    values = rows.astype(F32)
    scale = lax.rsqrt(jnp.mean(values * values, axis=-1, keepdims=True) + EPS)
    unit = values * scale
    return (unit * gain).astype(BF16), unit, scale


def dense_gates(routes, gates, experts):
    lane = jnp.arange(experts, dtype=jnp.int32)
    hit = (routes[:, :, None] == lane[None, None, :]).astype(F32)
    return hit, jnp.sum(hit * gates.astype(F32)[:, :, None], axis=1).astype(BF16)


def iota(shape, dim):
    return lax.broadcasted_iota(jnp.int32, shape, dim)


def ranks(table, tokens):
    rows = table.shape[0]
    taken = (table.astype(F32) > 0.0).astype(F32)
    row, col = iota((rows, rows), 0), iota((rows, rows), 1)
    upto = jnp.where((col <= row) & (col // tokens == row // tokens), 1.0, 0.0).astype(BF16)
    return mm(upto, taken.astype(BF16)) * taken


def pick_lane(array, lane):
    return jnp.sum(jnp.where(iota(array.shape, 1) == lane, array.astype(F32), 0.0), axis=1, keepdims=True)


def packing(table, lane, tokens):
    rows = table.shape[0]
    blocks = rows // tokens
    rank = pick_lane(ranks(table, tokens), lane)
    slot = iota((rows, blocks * CAP), 1)
    same = iota((rows, blocks * CAP), 0) // tokens == slot // CAP
    hit = same & (rank == ((slot % CAP) + 1).astype(F32))
    return jnp.where(hit, 1.0, 0.0).T.astype(BF16)


def backward_kernel(tokens, width, pos, gathered, wg, wu, wd, *rest):
    pieces, (d_gate_out, d_up_out, gated_out) = rest[:SIDE], rest[SIDE : SIDE + 3]
    held, wg_v, wu_v, wd_v, sems, weight_sems = rest[SIDE + 3 :]
    me, y = pos[0], pos[2]
    group = SIDE * tokens
    wide = held.shape[1]

    def source(d, zb):
        return (zb * SIDE + lax.rem(y + d, SIDE)) * tokens

    def block_copy(d, zb):
        return pltpu.make_async_copy(
            gathered.at[pl.ds(pl.multiple_of(source(d, zb), tokens), tokens), pl.ds(0, wide)],
            held.at[pl.ds(pl.multiple_of(d * group + zb * tokens, tokens), tokens), :],
            sems.at[d * SIDE + zb],
        )

    weights = [
        pltpu.make_async_copy(hbm, vmem, weight_sems.at[k])
        for k, (hbm, vmem) in enumerate(((wg, wg_v), (wu, wu_v), (wd, wd_v)))
    ]
    weights[0].start()
    for zb in range(SIDE):
        block_copy(0, zb).start()
    weights[1].start()
    weights[2].start()
    for d in range(1, SIDE):
        for zb in range(SIDE):
            block_copy(d, zb).start()
    for copy in weights:
        copy.wait()

    def tile(d, carry):
        for zb in range(SIDE):
            block_copy(d, zb).wait()
        at = pl.ds(pl.multiple_of(d * group, group), group)
        table = held[at, 2 * width :]
        gate = pick_lane(table, me)
        pack = packing(table, me, tokens)
        pre_gate = mm(held[at, :width], wg_v[...])
        pre_up = mm(held[at, :width], wu_v[...])
        plain = mm(held[at, width : 2 * width], wd_v[...], NT)
        sigma = jax.nn.sigmoid(pre_gate)
        active = pre_gate * sigma
        hidden = (active * pre_up).astype(BF16).astype(F32)
        d_hidden = plain * gate
        d_gate = (d_hidden * pre_up * sigma * (1.0 + pre_gate * (1.0 - sigma))).astype(BF16)
        d_up = (d_hidden * active).astype(BF16)
        gated = (hidden * gate).astype(BF16)
        dots = jnp.sum(hidden * plain, axis=1, keepdims=True)
        dots = jnp.where(iota((group, LANES), 1) == me, dots, 0.0).astype(BF16)
        for zb in range(SIDE):
            cut = slice(zb * tokens, (zb + 1) * tokens)
            to = pl.ds(pl.multiple_of(source(d, zb), tokens), tokens)
            d_gate_out[to, :] = d_gate[cut]
            d_up_out[to, :] = d_up[cut]
            gated_out[to, :] = gated[cut]
        gate_rows = mm(pack, d_gate).astype(BF16)
        up_rows = mm(pack, d_up).astype(BF16)
        dot_rows = mm(pack, dots).astype(BF16)
        grad = (mm(gate_rows, wg_v[...], NT) + mm(up_rows, wu_v[...], NT)).astype(BF16)
        for k in range(SIDE):

            @pl.when(d == k)
            def _():
                pieces[k][:, :width] = grad
                pieces[k][:, width:] = dot_rows

        return carry

    lax.fori_loop(0, SIDE, tile, 0)


def forward_kernel(tokens, width, offset, lane, pos, gathered, wg, wu, wd, *rest):
    pieces = rest[:SIDE]
    held, packed, wg_v, wu_v, wd_v, sems, weight_sems = rest[SIDE:]
    me, z = pos[0], pos[1]
    group = SIDE * tokens
    rows = SIDE * CAP
    wide = held.shape[1]

    def block_copy(d):
        start = pl.multiple_of(lax.rem(z + d, SIDE) * group, group)
        return pltpu.make_async_copy(
            gathered.at[pl.ds(start, group), pl.ds(offset, wide)],
            held.at[pl.ds(pl.multiple_of(d * group, group), group), :],
            sems.at[d],
        )

    weights = [
        pltpu.make_async_copy(hbm, vmem, weight_sems.at[k])
        for k, (hbm, vmem) in enumerate(((wg, wg_v), (wu, wu_v), (wd, wd_v)))
    ]
    for d in range(SIDE):
        block_copy(d).start()
    for copy in weights:
        copy.start()

    def pack_tile(d, carry):
        block_copy(d).wait()
        at = pl.ds(pl.multiple_of(d * group, group), group)
        pack = packing(held[at, :LANES], me + lane, tokens)
        to = pl.ds(pl.multiple_of(d * rows, rows), rows)
        packed[to, :] = mm(pack, held[at, LANES:]).astype(BF16)
        return carry

    lax.fori_loop(0, SIDE, pack_tile, 0)
    for copy in weights:
        copy.wait()

    def tile(c, carry):
        at = pl.ds(pl.multiple_of(c * 2 * rows, 2 * rows), 2 * rows)
        pre_gate = mm(packed[at, :], wg_v[...])
        pre_up = mm(packed[at, :], wu_v[...])
        hidden = (pre_gate * jax.nn.sigmoid(pre_gate) * pre_up).astype(BF16)
        out = mm(hidden, wd_v[...]).astype(BF16)
        for k in range(SIDE // 2):

            @pl.when(c == k)
            def _():
                pieces[2 * k][...] = out[:rows]
                pieces[2 * k + 1][...] = out[rows:]

        return carry

    lax.fori_loop(0, SIDE // 2, tile, 0)


def combine_kernel(tokens, along, offset, lane, weighted, pos, gathered, *rest):
    rows, outs, (tables, sems) = rest[:SIDE], rest[SIDE : 2 * SIDE], rest[2 * SIDE :]
    z, y = pos[1], pos[2]

    def block_of(d):
        return lax.rem((z if along == "y" else y) + d, SIDE)

    def copy(d):
        b = block_of(d)
        start = (b * SIDE + y) if along == "y" else (z * SIDE + b)
        return pltpu.make_async_copy(
            gathered.at[pl.ds(pl.multiple_of(start * tokens, tokens), tokens), pl.ds(offset, LANES)],
            tables.at[d],
            sems.at[d],
        )

    for d in range(SIDE):
        copy(d).start()
    column = iota((LANES, SIDE * CAP), 1)
    owner = jnp.zeros((LANES, SIDE * CAP), jnp.int32)
    for j in range(SIDE):
        if along == "y":
            expert = z * SIDE + lax.rem(y + SIDE - j, SIDE)
        else:
            expert = lax.rem(z + SIDE - j, SIDE) * SIDE + y
        owner = jnp.where(column // CAP == j, expert + lane, owner)
    spread = jnp.where(iota((LANES, SIDE * CAP), 0) == owner, 1.0, 0.0).astype(BF16)
    place = ((iota((tokens, SIDE * CAP), 1) % CAP) + 1).astype(F32)
    for d in range(SIDE):
        copy(d).wait()
        table = tables[d]
        here = mm(ranks(table, tokens).astype(BF16), spread) == place
        value = mm(table, spread) if weighted else 1.0
        matrix = jnp.where(here, value, 0.0).astype(BF16)
        at = pl.ds(pl.multiple_of(block_of(d) * CAP, CAP), CAP)
        mine = jnp.concatenate([part[at, :] for part in rows], axis=0)
        outs[d][...] = mm(matrix, mine).astype(BF16)


ANY = pl.BlockSpec(memory_space=pl.ANY)
VMEM = pl.BlockSpec(memory_space=pltpu.VMEM)
SMEM = pl.BlockSpec(memory_space=pltpu.SMEM)


def per_device(
    sent_acts,
    stash,
    cotangents,
    norm_gain,
    w_gate,
    w_up,
    w_down,
    routes_next,
    gates_next,
    routes_prev,
    gates_prev,
):
    experts = lax.axis_size("expert")
    me = lax.axis_index("expert")
    pos = jnp.stack([me, me // SIDE, me % SIDE]).astype(jnp.int32)
    gain = norm_gain[0].astype(F32)
    wg, wu, wd = w_gate[0, 0], w_up[0, 0], w_down[0, 0]
    tokens, width = sent_acts.shape[1:]
    ff = wg.shape[1]
    everyone = experts * tokens
    rows = SIDE * CAP
    params = pltpu.CompilerParams(vmem_limit_bytes=GRANT)

    cot = shifted(cotangents[0], "section", -1)
    arrived = shifted(sent_acts[0], "section", 1)
    prev_rows, unit_prev, scale_prev = rms_norm(stash[0], gain)
    hit_prev, table_prev = dense_gates(routes_prev[0], gates_prev[0], experts)
    _, table_next = dense_gates(routes_next[0], gates_next[0], experts)
    table = jnp.pad(jnp.concatenate([table_prev, table_next], axis=1), ((0, 0), (0, LANES - 2 * experts)))
    next_rows, _, _ = rms_norm(arrived, gain)
    bundle = jnp.concatenate([prev_rows, cot, table, next_rows], axis=1)
    gathered = lax.all_gather(bundle, "expert", axis=0, tiled=True)
    table_at = 2 * width

    weight_scratch = [
        pltpu.VMEM(wg.shape, BF16),
        pltpu.VMEM(wu.shape, BF16),
        pltpu.VMEM(wd.shape, BF16),
    ]
    unit = 2 * width * ff
    *pieces, d_gate, d_up, gated = pl.pallas_call(
        functools.partial(backward_kernel, tokens, width),
        out_shape=[jax.ShapeDtypeStruct((rows, width + LANES), BF16)] * SIDE
        + [jax.ShapeDtypeStruct((everyone, ff), BF16)] * 3,
        in_specs=[SMEM] + [ANY] * 4,
        out_specs=[VMEM] * (SIDE + 3),
        scratch_shapes=[pltpu.VMEM((everyone, 2 * width + LANES), BF16)]
        + weight_scratch
        + [pltpu.SemaphoreType.DMA((SIDE * SIDE,)), pltpu.SemaphoreType.DMA((3,))],
        compiler_params=params,
        cost_estimate=pl.CostEstimate(
            flops=(3 * everyone + 2 * SIDE * rows) * unit,
            bytes_accessed=26 * 1024 * 1024,
            transcendentals=everyone * ff,
        ),
        name="expert_backward",
    )(pos, gathered, wg, wu, wd)
    grads = [pull(pieces[d], "y", SIDE - d) for d in range(SIDE)]

    pieces = pl.pallas_call(
        functools.partial(forward_kernel, tokens, width, table_at, experts),
        out_shape=[jax.ShapeDtypeStruct((rows, width), BF16)] * SIDE,
        in_specs=[SMEM] + [ANY] * 4,
        out_specs=[VMEM] * SIDE,
        scratch_shapes=[
            pltpu.VMEM((everyone, width + LANES), BF16),
            pltpu.VMEM((SIDE * rows, width), BF16),
        ]
        + weight_scratch
        + [pltpu.SemaphoreType.DMA((SIDE,)), pltpu.SemaphoreType.DMA((3,))],
        compiler_params=params,
        cost_estimate=pl.CostEstimate(
            flops=3 * SIDE * rows * unit, bytes_accessed=18 * 1024 * 1024, transcendentals=SIDE * rows * ff
        ),
        name="expert_forward",
    )(pos, gathered, wg, wu, wd)
    outs = [pull(pieces[d], "z", SIDE - d) for d in range(SIDE)]

    def combine(parts, along, lane, weighted):
        wide = parts[0].shape[1]
        return pl.pallas_call(
            functools.partial(combine_kernel, tokens, along, table_at, lane, weighted),
            out_shape=[jax.ShapeDtypeStruct((tokens, wide), BF16)] * SIDE,
            in_specs=[SMEM, ANY] + [VMEM] * SIDE,
            out_specs=[VMEM] * SIDE,
            scratch_shapes=[pltpu.VMEM((SIDE, tokens, LANES), BF16), pltpu.SemaphoreType.DMA((SIDE,))],
            compiler_params=params,
            cost_estimate=pl.CostEstimate(
                flops=2 * SIDE * tokens * rows * wide, bytes_accessed=5 * 1024 * 1024, transcendentals=0
            ),
            name="combine_" + along,
        )(pos, gathered, *parts)

    partial = combine(grads, "y", 0, False)
    summed = sum(pull(partial[d], "z", SIDE - d).astype(F32) for d in range(SIDE))
    partial = combine(outs, "z", experts, True)
    mixed = sum(pull(partial[d], "y", SIDE - d).astype(F32) for d in range(SIDE))
    fwd_out = (arrived.astype(F32) + mixed).astype(BF16)

    grad_gate = mm(gathered[:, :width], d_gate, TN).astype(BF16)
    grad_up = mm(gathered[:, :width], d_up, TN).astype(BF16)
    grad_down = mm(gated, gathered[:, width : 2 * width], TN).astype(BF16)

    gate_grad = jnp.sum(hit_prev * summed[:, None, width : width + experts], axis=2).astype(BF16)
    dxhat = summed[:, :width] * gain
    bwd_out = cot.astype(F32) + scale_prev * (
        dxhat - unit_prev * jnp.mean(dxhat * unit_prev, axis=-1, keepdims=True)
    )
    return (
        fwd_out[None],
        bwd_out.astype(BF16)[None],
        gate_grad[None],
        grad_gate[None, None],
        grad_up[None, None],
        grad_down[None, None],
    )


def solution(mesh):
    tokens = P("section", "expert", None)
    weight = P("section", "expert", None, None)
    return jax.shard_map(
        per_device,
        mesh=mesh,
        in_specs=(tokens, tokens, tokens, P("section", None), weight, weight, weight, tokens, tokens, tokens, tokens),
        out_specs=(tokens, tokens, tokens, weight, weight, weight),
        check_vma=False,
    )
```

time: 290 us -> 230 us (0.79)
  blocking collectives: 57.8 us -> 0 us
  matrix products: 74.8 us -> 21.9 us
  Pallas kernels: 0 us -> 50.3 us
  waiting for transfers between devices: 102 us -> 113 us
  other arithmetic: 14.3 us -> 9.79 us
  local copies, waits for them, and re-layouts: 4.71 us -> 0.29 us
    all_gather x1 -> x0, blocking collectives: 57.8 us -> none  [per_device(): lax.all_gather(token_dots, 'expert', axis=0, tiled=True)]
    dot_general x16 -> x3, matrix products: 74 us -> 21.9 us  [mm(): return lax.dot_general(a, b, (dims, ((), ())), preferred_element_type=F32)]
    pallas_call x0 -> x4, Pallas kernels: none -> 50.3 us  [the longest x1 29.5 us: per_device(): pl.pallas_call(functools.partial(backward_kernel, tokens, width), out_sha...]
    all_to_all x3 -> x0, waiting for transfers between devices: 49.7 us -> none  [the longest x1 49.7 us: per_device(): lax.all_to_all(send.reshape(experts, CAP, width), 'expert', split_axis=0,...]
    all_gather x1, waiting for transfers between devices: 47 us -> 92.7 us  [per_device(): gathered = lax.all_gather(bundle, 'expert', axis=0, tiled=True)]
    ppermute x0 -> x12, waiting for transfers between devices: none -> 20.7 us  [pull(): return lax.ppermute(array, 'expert', pairs)]
    all_to_all x3 -> x0, starting transfers between devices: 18.8 us -> none  [the longest x1 8.09 us: per_device(): lax.all_to_all(send.reshape(experts, CAP, width), 'expert', split_axis=0,...]
    ppermute x0 -> x12, starting transfers between devices: none -> 16.7 us  [pull(): return lax.ppermute(array, 'expert', pairs)]
  transfers between devices with their start and end apart: 6 -> 15, of which waited for: 3 -> 4; matrix products, arithmetic and copies ran while one was open for 30% -> 13% of each run, Pallas kernels for 0% -> 16%
where the time goes in v1:
time: 230 us
  waiting for transfers between devices  113 us (49%)
  Pallas kernels  50.3 us (22%)
  matrix products  21.9 us (10%)
  starting transfers between devices  19.7 us (9%)
  between operations  14.2 us (6%)
  other arithmetic  9.79 us (4%)
    all_gather x1, waiting for transfers between devices, per_device(): gathered = lax.all_gather(bundle, 'expert', axis=0, tiled=True)  92.7 us
    pallas_call x1, Pallas kernels, per_device(): pl.pallas_call(functools.partial(backward_kernel, tokens, width), out_sha...  29.5 us
    dot_general x3, matrix products, mm(): return lax.dot_general(a, b, (dims, ((), ())), preferred_element_type=F32)  21.9 us
    ppermute x12, waiting for transfers between devices, pull(): return lax.ppermute(array, 'expert', pairs)  20.7 us
    ppermute x12, starting transfers between devices, pull(): return lax.ppermute(array, 'expert', pairs)  16.7 us
    pallas_call x1, Pallas kernels, per_device(): pl.pallas_call(functools.partial(forward_kernel, tokens, width, table_at,...  14.2 us
    pallas_call x2, Pallas kernels, combine(): pl.pallas_call(functools.partial(combine_kernel, tokens, along, table_at,...  6.61 us
  transfers between devices with their start and end apart: 15, of which 4 were waited for; matrix products, arithmetic and copies ran while one was open for 13% of the time, Pallas kernels for 16%

profile of v1, /device:TPU:0, one launch (start us, length us, event | category | flops | bytes accessed | tf_op | source)
XLA Modules:
  0.0 229.6 jit_solution(3575622316920380845)
XLA Ops:
  7.2 2.9 %collective-permute-start.1 = (bf16[64,2048]{1,0:T(8,128)(2,1)}, bf16[64,2048]{1,0:T(8,128)(2,1)S(1)}, u32[]{:S(2)}, u32[]{:S(2)}) collective-permute-start(bf16[64,2048]{1,0:T(8,128)(2,1)} %bitcast.53), channel_id=1, source_target_pairs={{0,112},{16,0},{32,16},{48,32},{64,48},{80,64},{96,80},{112,96},{1... | collective-permute-start | bytes 786440 | tf_op jit(solution)/shard_map/ppermute | solution.py:25
  10.2 1.1 fusion.33
  11.3 0.7 bitcast_convert_fusion
  12.0 0.7 bitcast_convert_fusion.1
  12.7 0.7 select_reduce_fusion.2
  13.5 0.7 select_reduce_fusion.1
  14.4 0.7 mul.110
  15.3 1.1 fusion.27
  16.4 0.9 pad_maximum_fusion
  17.5 92.7 %all-gather.2.cloned.1.call-done.gathered = bf16[1024,6272]{1,0:T(8,128)(2,1)} async-done(((bf16[64,6272]{1,0:T(8,128)(2,1)}), bf16[1024,6272]{1,0:T(8,128)(2,1)}) %all-gather.2.cloned.1.call-update) | async-done | bytes 12845072 | tf_op jit(solution)/shard_map/all_gather | solution.py:286
  110.2 14.2 %expert_forward.1 = (bf16[192,2048]{1,0:T(8,128)(2,1)S(1)}, bf16[192,2048]{1,0:T(8,128)(2,1)S(1)}, bf16[192,2048]{1,0:T(8,128)(2,1)S(1)}, bf16[192,2048]{1,0:T(8,128)(2,1)S(1)}) custom-call(s32[3]{0:T(128)S(1)} %pad_add_fusion.pos, bf16[1024,6272]{1,0:T(8,128)(2,1)} %all-gather.2.cloned.1.call-done.gathered, bf16[2048,768]{1,0:T(8,128)(2,1)} %bitcast.46, ...), custom_call_target="tpu_custom_call" | custom-call | flops 7247757312 | bytes 18874368 | tf_op jit(solution)/shard_map/expert_forward/pallas_call | solution.py:314
  124.3 1.4 collective-permute-start.2
  125.7 2.9 %collective-permute-start.3 = (bf16[192,2048]{1,0:T(8,128)(2,1)S(1)}, bf16[192,2048]{1,0:T(8,128)(2,1)S(1)}, u32[]{:S(2)}, u32[]{:S(2)}) collective-permute-start(bf16[192,2048]{1,0:T(8,128)(2,1)S(1)} %get-tuple-element.27), channel_id=1, source_target_pairs={{8,0},{9,1},{10,2},{11,3},{12,4},{13,5},{14,6},{15,7},{0,8},{1,9},... | collective-permute-start | bytes 2359304 | tf_op jit(solution)/shard_map/ppermute | solution.py:36
  128.6 1.4 collective-permute-start.4
  130.0 29.5 %expert_backward.1 = (bf16[192,2176]{1,0:T(8,128)(2,1)S(1)}, bf16[192,2176]{1,0:T(8,128)(2,1)S(1)}, bf16[192,2176]{1,0:T(8,128)(2,1)S(1)}, bf16[192,2176]{1,0:T(...) custom-call(s32[3]{0:T(128)S(1)} %pad_add_fusion.pos, ...), custom_call_target="tpu_custom_call" | custom-call | flops 14495514624 | bytes 27262976 | tf_op jit(solution)/shard_map/expert_backward/pallas_call | solution.py:295
  159.8 2.5 %collective-permute-start.9 = (bf16[192,2176]{1,0:T(8,128)(2,1)S(1)}, bf16[192,2176]{1,0:T(8,128)(2,1)S(1)}, u32[]{:S(2)}, u32[]{:S(2)}) collective-permute-start(bf16[192,2176]{1,0:T(8,128)(2,1)S(1)} %get-tuple-element.35), channel_id=1, source_target_pairs={{2,0},{3,1},{0,2},{1,3},{6,4},{7,5},{4,6},{5,7},{10,8},{11,9},{8,1... | collective-permute-start | bytes 2506760 | tf_op jit(solution)/shard_map/ppermute | solution.py:36
  162.3 7.5 %fusion.21 = bf16[1,1,2048,768]{3,2,1,0:T(8,128)(2,1)} fusion(bf16[1024,768]{1,0:T(8,128)(2,1)S(1)} %get-tuple-element.41, bf16[1024,6272]{1,0:T(8,128)(2,1)} %all-gather.2.cloned.1.call-done.gathered), kind=kOutput, calls=%fused_computation.11 | convolution fusion | flops 3222798336 | bytes 8912896 | tf_op jit(solution)/shard_map/dot_general | solution.py:40
  169.8 1.5 collective-permute-start.10
  171.3 7.4 %fusion.18 = bf16[1,1,2048,768]{3,2,1,0:T(8,128)(2,1)} fusion(bf16[1024,768]{1,0:T(8,128)(2,1)S(1)} %copy-done.3, bf16[1024,6272]{1,0:T(8,128)(2,1)} %all-gather.2.cloned.1.call-done.gathered), kind=kOutput, calls=%fused_computation.10 | convolution fusion | flops 3222798336 | bytes 8912896 | tf_op jit(solution)/shard_map/dot_general | solution.py:40
  178.7 3.2 %combine_z.1 = (bf16[64,2048]{1,0:T(8,128)(2,1)S(1)}, bf16[64,2048]{1,0:T(8,128)(2,1)S(1)}, bf16[64,2048]{1,0:T(8,128)(2,1)S(1)}, bf16[64,2048]{1,0:T(8,128)(2,1)S(1)}) custom-call(s32[3]{0:T(128)S(1)} %pad_add_fusion.pos, bf16[1024,6272]{1,0:T(8,128)(2,1)} %all-gather.2.cloned.1.call-done.gathered, bf16[192,2048]{1,0:T(8,128)(2,1)S(1)} %get-tuple-element.25.rest_0_, ...), custom_call_target="tpu_custom_call" | custom-call | flops 201326592 | bytes 5242880 | tf_op jit(solution)/shard_map/combine_z/pallas_call | solution.py:335
  181.9 0.6 collective-permute-start.5
  182.5 1.5 collective-permute-start.6
  184.1 13.2 %collective-permute-done.8.rest_1_ = bf16[192,2176]{1,0:T(8,128)(2,1)S(1)} collective-permute-done((bf16[192,2176]{1,0:T(8,128)(2,1)S(1)}, bf16[192,2176]{1,0:T(8,128)(2,1)S(1)}, u32[]{:S(2)}, u32[]{:S(2)}) %collective-permute-start.8) | collective-permute-done | bytes 835616 | tf_op jit(solution)/shard_map/ppermute | solution.py:36
  197.3 7.0 %fusion.15 = bf16[1,1,768,2048]{3,2,1,0:T(8,128)(2,1)} fusion(bf16[1024,768]{1,0:T(8,128)(2,1)S(1)} %copy-done.2, bf16[1024,6272]{1,0:T(8,128)(2,1)} %all-gather.2.cloned.1.call-done.gathered), kind=kOutput, calls=%fused_computation.9 | convolution fusion | flops 3222798336 | bytes 8912896 | tf_op jit(solution)/shard_map/dot_general | solution.py:40
  204.3 3.4 %combine_y.1 = (bf16[64,2176]{1,0:T(8,128)(2,1)S(1)}, bf16[64,2176]{1,0:T(8,128)(2,1)S(1)}, bf16[64,2176]{1,0:T(8,128)(2,1)S(1)}, bf16[64,2176]{1,0:T(8,128)(2,1)S(1)}) custom-call(s32[3]{0:T(128)S(1)} %pad_add_fusion.pos, bf16[1024,6272]{1,0:T(8,128)(2,1)} %all-gather.2.cloned.1.call-done.gathered, bf16[192,2176]{1,0:T(8,128)(2,1)S(1)} %get-tuple-element.33.rest_0_, ...), custom_call_target="tpu_custom_call" | custom-call | flops 213909504 | bytes 5242880 | tf_op jit(solution)/shard_map/combine_y/pallas_call | solution.py:335
  207.7 1.9 collective-permute-start.11
  209.6 2.8 %collective-permute-start.13 = (bf16[64,2176]{1,0:T(8,128)(2,1)S(1)}, bf16[64,2176]{1,0:T(8,128)(2,1)S(1)}, u32[]{:S(2)}, u32[]{:S(2)}) collective-permute-start(bf16[64,2176]{1,0:T(8,128)(2,1)S(1)} %get-tuple-element.40), channel_id=1, source_target_pairs={{4,0},{5,1},{6,2},{7,3},{8,4},{9,5},{10,6},{11,7},{12,8},{13,9},{1... | collective-permute-start | bytes 835592 | tf_op jit(solution)/shard_map/ppermute | solution.py:36
  212.4 0.9 fusion.38
  213.3 5.4 %collective-permute-done.11 = bf16[64,2176]{1,0:T(8,128)(2,1)S(1)} collective-permute-done((bf16[64,2176]{1,0:T(8,128)(2,1)S(1)}, bf16[64,2176]{1,0:T(8,128)(2,1)S(1)}, u32[]{:S(2)}, u32[]{:S(2)}) %collective-permute-start.11) | collective-permute-done | bytes 278560 | tf_op jit(solution)/shard_map/ppermute | solution.py:36
  218.7 2.1 collective-permute-done.13
  221.2 0.6 select_reduce_fusion
  221.9 0.9 fusion.39
  (37 shorter events, 1.4 us)
Async XLA Ops:
  7.2 103.0 %all-gather.2.cloned.1.call-start = ((), (), s32[]{:S(2)}) async-start(), calls=%async_computation | async-start | bytes 13647872 | tf_op jit(solution)/shard_map/all_gather | solution.py:286
  7.2 7.9 %collective-permute-start = (bf16[64,2048]{1,0:T(8,128)(2,1)}, bf16[64,2048]{1,0:T(8,128)(2,1)S(1)}, u32[]{:S(2)}, u32[]{:S(2)}) collective-permute-start(bf16[64,2048]{1,0:T(8,128)(2,1)} %bitcast.52), channel_id=1, source_target_pairs={{0,16},{16,32},{32,48},{48,64},{64,80},{80,96},{96,112},{112,0},{1... | collective-permute-start | bytes 786440 | tf_op jit(solution)/shard_map/ppermute | solution.py:25
  7.2 9.2 %collective-permute-start.1 = (bf16[64,2048]{1,0:T(8,128)(2,1)}, bf16[64,2048]{1,0:T(8,128)(2,1)S(1)}, u32[]{:S(2)}, u32[]{:S(2)}) collective-permute-start(bf16[64,2048]{1,0:T(8,128)(2,1)} %bitcast.53), channel_id=1, source_target_pairs={{0,112},{16,0},{32,16},{48,32},{64,48},{80,64},{96,80},{112,96},{1... | collective-permute-start | bytes 786440 | tf_op jit(solution)/shard_map/ppermute | solution.py:25
  124.3 45.5 %collective-permute-start.2 = (bf16[192,2048]{1,0:T(8,128)(2,1)S(1)}, bf16[192,2048]{1,0:T(8,128)(2,1)S(1)}, u32[]{:S(2)}, u32[]{:S(2)}) collective-permute-start(bf16[192,2048]{1,0:T(8,128)(2,1)S(1)} %get-tuple-element.26), channel_id=1, source_target_pairs={{12,0},{13,1},{14,2},{15,3},{0,4},{1,5},{2,6},{3,7},{4,8},{5,9},{6... | collective-permute-start | bytes 2359304 | tf_op jit(solution)/shard_map/ppermute | solution.py:36
  125.7 52.9 %collective-permute-start.3 = (bf16[192,2048]{1,0:T(8,128)(2,1)S(1)}, bf16[192,2048]{1,0:T(8,128)(2,1)S(1)}, u32[]{:S(2)}, u32[]{:S(2)}) collective-permute-start(bf16[192,2048]{1,0:T(8,128)(2,1)S(1)} %get-tuple-element.27), channel_id=1, source_target_pairs={{8,0},{9,1},{10,2},{11,3},{12,4},{13,5},{14,6},{15,7},{0,8},{1,9},... | collective-permute-start | bytes 2359304 | tf_op jit(solution)/shard_map/ppermute | solution.py:36
  128.6 50.1 %collective-permute-start.4 = (bf16[192,2048]{1,0:T(8,128)(2,1)S(1)}, bf16[192,2048]{1,0:T(8,128)(2,1)S(1)}, u32[]{:S(2)}, u32[]{:S(2)}) collective-permute-start(bf16[192,2048]{1,0:T(8,128)(2,1)S(1)} %get-tuple-element.28), channel_id=1, source_target_pairs={{4,0},{5,1},{6,2},{7,3},{8,4},{9,5},{10,6},{11,7},{12,8},{13,9},{1... | collective-permute-start | bytes 2359304 | tf_op jit(solution)/shard_map/ppermute | solution.py:36
  159.5 37.8 %collective-permute-start.8 = (bf16[192,2176]{1,0:T(8,128)(2,1)S(1)}, bf16[192,2176]{1,0:T(8,128)(2,1)S(1)}, u32[]{:S(2)}, u32[]{:S(2)}) collective-permute-start(bf16[192,2176]{1,0:T(8,128)(2,1)S(1)} %get-tuple-element.34), channel_id=1, source_target_pairs={{3,0},{0,1},{1,2},{2,3},{7,4},{4,5},{5,6},{6,7},{11,8},{8,9},{9,10... | collective-permute-start | bytes 2506760 | tf_op jit(solution)/shard_map/ppermute | solution.py:36
  159.8 44.5 %collective-permute-start.9 = (bf16[192,2176]{1,0:T(8,128)(2,1)S(1)}, bf16[192,2176]{1,0:T(8,128)(2,1)S(1)}, u32[]{:S(2)}, u32[]{:S(2)}) collective-permute-start(bf16[192,2176]{1,0:T(8,128)(2,1)S(1)} %get-tuple-element.35), channel_id=1, source_target_pairs={{2,0},{3,1},{0,2},{1,3},{6,4},{7,5},{4,6},{5,7},{10,8},{11,9},{8,1... | collective-permute-start | bytes 2506760 | tf_op jit(solution)/shard_map/ppermute | solution.py:36
  162.3 9.0 %copy-start.3 = (bf16[1024,768]{1,0:T(8,128)(2,1)S(1)}, bf16[1024,768]{1,0:T(8,128)(2,1)}, u32[]{:S(2)}) copy-start(bf16[1024,768]{1,0:T(8,128)(2,1)} %get-tuple-element.42) | copy-start | bytes 4718596
  169.8 34.5 %collective-permute-start.10 = (bf16[192,2176]{1,0:T(8,128)(2,1)S(1)}, bf16[192,2176]{1,0:T(8,128)(2,1)S(1)}, u32[]{:S(2)}, u32[]{:S(2)}) collective-permute-start(bf16[192,2176]{1,0:T(8,128)(2,1)S(1)} %get-tuple-element.36), channel_id=1, source_target_pairs={{1,0},{2,1},{3,2},{0,3},{5,4},{6,5},{7,6},{4,7},{9,8},{10,9},{11,1... | collective-permute-start | bytes 2506760 | tf_op jit(solution)/shard_map/ppermute | solution.py:36
  178.7 18.6 %copy-start.2 = (bf16[1024,768]{1,0:T(8,128)(2,1)S(1)}, bf16[1024,768]{1,0:T(8,128)(2,1)}, u32[]{:S(2)}) copy-start(bf16[1024,768]{1,0:T(8,128)(2,1)} %get-tuple-element.43) | copy-start | bytes 4718596
  181.9 27.7 %collective-permute-start.5 = (bf16[64,2048]{1,0:T(8,128)(2,1)S(1)}, bf16[64,2048]{1,0:T(8,128)(2,1)S(1)}, u32[]{:S(2)}, u32[]{:S(2)}) collective-permute-start(bf16[64,2048]{1,0:T(8,128)(2,1)S(1)} %get-tuple-element.30), channel_id=1, source_target_pairs={{3,0},{0,1},{1,2},{2,3},{7,4},{4,5},{5,6},{6,7},{11,8},{8,9},{9,10... | collective-permute-start | bytes 786440 | tf_op jit(solution)/shard_map/ppermute | solution.py:36
  182.5 29.9 %collective-permute-start.6 = (bf16[64,2048]{1,0:T(8,128)(2,1)S(1)}, bf16[64,2048]{1,0:T(8,128)(2,1)S(1)}, u32[]{:S(2)}, u32[]{:S(2)}) collective-permute-start(bf16[64,2048]{1,0:T(8,128)(2,1)S(1)} %get-tuple-element.31), channel_id=1, source_target_pairs={{2,0},{3,1},{0,2},{1,3},{6,4},{7,5},{4,6},{5,7},{10,8},{11,9},{8,1... | collective-permute-start | bytes 786440 | tf_op jit(solution)/shard_map/ppermute | solution.py:36
  197.3 15.1 %collective-permute-start.7 = (bf16[64,2048]{1,0:T(8,128)(2,1)S(1)}, bf16[64,2048]{1,0:T(8,128)(2,1)S(1)}, u32[]{:S(2)}, u32[]{:S(2)}) collective-permute-start(bf16[64,2048]{1,0:T(8,128)(2,1)S(1)} %get-tuple-element.32), channel_id=1, source_target_pairs={{1,0},{2,1},{3,2},{0,3},{5,4},{6,5},{7,6},{4,7},{9,8},{10,9},{11,1... | collective-permute-start | bytes 786440 | tf_op jit(solution)/shard_map/ppermute | solution.py:36
  207.7 13.2 %copy-start = (bf16[1,64,2048]{2,1,0:T(8,128)(2,1)S(1)}, bf16[1,64,2048]{2,1,0:T(8,128)(2,1)}, u32[]{:S(2)}) copy-start(bf16[1,64,2048]{2,1,0:T(8,128)(2,1)} %param.12) | copy-start | bytes 786436
  207.7 13.5 %copy-start.1 = (s32[1,64,8]{1,2,0:T(8,128)S(1)}, s32[1,64,8]{1,2,0:T(8,128)}, u32[]{:S(2)}) copy-start(s32[1,64,8]{1,2,0:T(8,128)} %param.20) | copy-start | bytes 6148
  207.7 10.9 %collective-permute-start.11 = (bf16[64,2176]{1,0:T(8,128)(2,1)S(1)}, bf16[64,2176]{1,0:T(8,128)(2,1)S(1)}, u32[]{:S(2)}, u32[]{:S(2)}) collective-permute-start(bf16[64,2176]{1,0:T(8,128)(2,1)S(1)} %get-tuple-element.38), channel_id=1, source_target_pairs={{12,0},{13,1},{14,2},{15,3},{0,4},{1,5},{2,6},{3,7},{4,8},{5,9},{6... | collective-permute-start | bytes 835592 | tf_op jit(solution)/shard_map/ppermute | solution.py:36
  209.6 9.0 %collective-permute-start.12 = (bf16[64,2176]{1,0:T(8,128)(2,1)S(1)}, bf16[64,2176]{1,0:T(8,128)(2,1)S(1)}, u32[]{:S(2)}, u32[]{:S(2)}) collective-permute-start(bf16[64,2176]{1,0:T(8,128)(2,1)S(1)} %get-tuple-element.39), channel_id=1, source_target_pairs={{8,0},{9,1},{10,2},{11,3},{12,4},{13,5},{14,6},{15,7},{0,8},{1,9},... | collective-permute-start | bytes 835592 | tf_op jit(solution)/shard_map/ppermute | solution.py:36
  209.6 11.1 %collective-permute-start.13 = (bf16[64,2176]{1,0:T(8,128)(2,1)S(1)}, bf16[64,2176]{1,0:T(8,128)(2,1)S(1)}, u32[]{:S(2)}, u32[]{:S(2)}) collective-permute-start(bf16[64,2176]{1,0:T(8,128)(2,1)S(1)} %get-tuple-element.40), channel_id=1, source_target_pairs={{4,0},{5,1},{6,2},{7,3},{8,4},{9,5},{10,6},{11,7},{12,8},{13,9},{1... | collective-permute-start | bytes 835592 | tf_op jit(solution)/shard_map/ppermute | solution.py:36
Sparse Core Ops, SparseCore 0:
  17.5 92.6 all-gather.1

commit v2 on v1

--- a/solution.py
+++ b/solution.py
@@ -79,93 +79,98 @@
     return jnp.where(hit, 1.0, 0.0).T.astype(BF16)
 
 
-def backward_kernel(tokens, width, pos, gathered, wg, wu, wd, *rest):
-    pieces, (d_gate_out, d_up_out, gated_out) = rest[:SIDE], rest[SIDE : SIDE + 3]
-    held, wg_v, wu_v, wd_v, sems, weight_sems = rest[SIDE + 3 :]
-    me, y = pos[0], pos[2]
+def weight_copies(refs, held, sems):
+    return [pltpu.make_async_copy(hbm, vmem, sems.at[k]) for k, (hbm, vmem) in enumerate(zip(refs, held))]
+
+
+def pack_lines(tokens, table, lane, out, rows):
     group = SIDE * tokens
-    wide = held.shape[1]
-
-    def source(d, zb):
-        return (zb * SIDE + lax.rem(y + d, SIDE)) * tokens
-
-    def block_copy(d, zb):
+    count = SIDE * CAP
+    gates = []
+    for k in range(table.shape[0] // group):
+        at = slice(k * group, (k + 1) * group)
+        pack = packing(table[at, :], lane, tokens)
+        out[k * count : (k + 1) * count, :] = mm(pack, rows[at, :]).astype(BF16)
+        gates.append(pick_lane(mm(pack, table[at, :]), lane))
+    return jnp.concatenate(gates, axis=0)
+
+
+def backward_kernel(tokens, width, pos, both, table, wg, wu, wd, *rest):
+    pieces, (d_gate_out, d_up_out, gated_out, packed) = rest[:SIDE], rest[SIDE : SIDE + 4]
+    grads, wg_v, wu_v, wd_v, sems, piece_sems = rest[SIDE + 4 :]
+    me, z = pos[0], pos[1]
+    step = pl.program_id(0)
+    first = step == 0
+    slots = packed.shape[0]
+    lines = slots // (SIDE * CAP)
+
+    def piece_copy(k):
+        source = lax.rem(z + k, SIDE) * SIDE * CAP
         return pltpu.make_async_copy(
-            gathered.at[pl.ds(pl.multiple_of(source(d, zb), tokens), tokens), pl.ds(0, wide)],
-            held.at[pl.ds(pl.multiple_of(d * group + zb * tokens, tokens), tokens), :],
-            sems.at[d * SIDE + zb],
+            grads.at[pl.ds(pl.multiple_of(source, SIDE * CAP), SIDE * CAP), :], pieces[k], piece_sems.at[k]
         )
 
-    weights = [
-        pltpu.make_async_copy(hbm, vmem, weight_sems.at[k])
-        for k, (hbm, vmem) in enumerate(((wg, wg_v), (wu, wu_v), (wd, wd_v)))
-    ]
-    weights[0].start()
-    for zb in range(SIDE):
-        block_copy(0, zb).start()
-    weights[1].start()
-    weights[2].start()
-    for d in range(1, SIDE):
-        for zb in range(SIDE):
-            block_copy(d, zb).start()
-    for copy in weights:
-        copy.wait()
-
-    def tile(d, carry):
-        for zb in range(SIDE):
-            block_copy(d, zb).wait()
-        at = pl.ds(pl.multiple_of(d * group, group), group)
-        table = held[at, 2 * width :]
-        gate = pick_lane(table, me)
-        pack = packing(table, me, tokens)
-        pre_gate = mm(held[at, :width], wg_v[...])
-        pre_up = mm(held[at, :width], wu_v[...])
-        plain = mm(held[at, width : 2 * width], wd_v[...], NT)
-        sigma = jax.nn.sigmoid(pre_gate)
-        active = pre_gate * sigma
-        hidden = (active * pre_up).astype(BF16).astype(F32)
-        d_hidden = plain * gate
-        d_gate = (d_hidden * pre_up * sigma * (1.0 + pre_gate * (1.0 - sigma))).astype(BF16)
-        d_up = (d_hidden * active).astype(BF16)
-        gated = (hidden * gate).astype(BF16)
-        dots = jnp.sum(hidden * plain, axis=1, keepdims=True)
-        dots = jnp.where(iota((group, LANES), 1) == me, dots, 0.0).astype(BF16)
-        for zb in range(SIDE):
-            cut = slice(zb * tokens, (zb + 1) * tokens)
-            to = pl.ds(pl.multiple_of(source(d, zb), tokens), tokens)
-            d_gate_out[to, :] = d_gate[cut]
-            d_up_out[to, :] = d_up[cut]
-            gated_out[to, :] = gated[cut]
-        gate_rows = mm(pack, d_gate).astype(BF16)
-        up_rows = mm(pack, d_up).astype(BF16)
-        dot_rows = mm(pack, dots).astype(BF16)
-        grad = (mm(gate_rows, wg_v[...], NT) + mm(up_rows, wu_v[...], NT)).astype(BF16)
+    copies = weight_copies((wg, wu, wd), (wg_v, wu_v, wd_v), sems)
+
+    @pl.when(first)
+    def _():
+        for copy in copies:
+            copy.start()
+
+    gate = pack_lines(tokens, table, me, packed, both)
+
+    @pl.when(first)
+    def _():
+        copies[0].wait()
+
+    pre_gate = mm(packed[:, :width], wg_v[...])
+
+    @pl.when(first)
+    def _():
+        copies[1].wait()
+        copies[2].wait()
+
+    pre_up = mm(packed[:, :width], wu_v[...])
+    plain = mm(packed[:, width:], wd_v[...], NT)
+    sigma = jax.nn.sigmoid(pre_gate)
+    active = pre_gate * sigma
+    hidden = (active * pre_up).astype(BF16).astype(F32)
+    d_hidden = plain * gate
+    d_gate = (d_hidden * pre_up * sigma * (1.0 + pre_gate * (1.0 - sigma))).astype(BF16)
+    d_up = (d_hidden * active).astype(BF16)
+    d_gate_out[...] = d_gate
+    d_up_out[...] = d_up
+    gated_out[...] = (hidden * gate).astype(BF16)
+    dots = jnp.sum(hidden * plain, axis=1, keepdims=True)
+    here = pl.ds(pl.multiple_of(step * slots, slots), slots)
+    grads[here, width:] = jnp.where(iota((slots, LANES), 1) == me, dots, 0.0).astype(BF16)
+    grads[here, :width] = (mm(d_gate, wg_v[...], NT) + mm(d_up, wu_v[...], NT)).astype(BF16)
+    for k in range(SIDE):
+
+        @pl.when(lax.rem(z + k, SIDE) // lines == step)
+        def _():
+            piece_copy(k).start()
+
+    @pl.when(step == pl.num_programs(0) - 1)
+    def _():
         for k in range(SIDE):
-
-            @pl.when(d == k)
-            def _():
-                pieces[k][:, :width] = grad
-                pieces[k][:, width:] = dot_rows
-
-        return carry
-
-    lax.fori_loop(0, SIDE, tile, 0)
+            piece_copy(k).wait()
 
 
 def forward_kernel(tokens, width, offset, lane, pos, gathered, wg, wu, wd, *rest):
     pieces = rest[:SIDE]
     held, packed, wg_v, wu_v, wd_v, sems, weight_sems = rest[SIDE:]
-    me, z = pos[0], pos[1]
+    me, y = pos[0], pos[2]
     group = SIDE * tokens
     rows = SIDE * CAP
     wide = held.shape[1]
 
-    def block_copy(d):
-        start = pl.multiple_of(lax.rem(z + d, SIDE) * group, group)
+    def block_copy(d, zb):
+        start = pl.multiple_of((zb * SIDE + lax.rem(y + d, SIDE)) * tokens, tokens)
         return pltpu.make_async_copy(
-            gathered.at[pl.ds(start, group), pl.ds(offset, wide)],
-            held.at[pl.ds(pl.multiple_of(d * group, group), group), :],
-            sems.at[d],
+            gathered.at[pl.ds(start, tokens), pl.ds(offset, wide)],
+            held.at[pl.ds(pl.multiple_of(d * group + zb * tokens, tokens), tokens), :],
+            sems.at[d * SIDE + zb],
         )
 
     weights = [
@@ -173,12 +178,14 @@
         for k, (hbm, vmem) in enumerate(((wg, wg_v), (wu, wu_v), (wd, wd_v)))
     ]
     for d in range(SIDE):
-        block_copy(d).start()
+        for zb in range(SIDE):
+            block_copy(d, zb).start()
     for copy in weights:
         copy.start()
 
     def pack_tile(d, carry):
-        block_copy(d).wait()
+        for zb in range(SIDE):
+            block_copy(d, zb).wait()
         at = pl.ds(pl.multiple_of(d * group, group), group)
         pack = packing(held[at, :LANES], me + lane, tokens)
         to = pl.ds(pl.multiple_of(d * rows, rows), rows)
@@ -292,25 +299,6 @@
         pltpu.VMEM(wd.shape, BF16),
     ]
     unit = 2 * width * ff
-    *pieces, d_gate, d_up, gated = pl.pallas_call(
-        functools.partial(backward_kernel, tokens, width),
-        out_shape=[jax.ShapeDtypeStruct((rows, width + LANES), BF16)] * SIDE
-        + [jax.ShapeDtypeStruct((everyone, ff), BF16)] * 3,
-        in_specs=[SMEM] + [ANY] * 4,
-        out_specs=[VMEM] * (SIDE + 3),
-        scratch_shapes=[pltpu.VMEM((everyone, 2 * width + LANES), BF16)]
-        + weight_scratch
-        + [pltpu.SemaphoreType.DMA((SIDE * SIDE,)), pltpu.SemaphoreType.DMA((3,))],
-        compiler_params=params,
-        cost_estimate=pl.CostEstimate(
-            flops=(3 * everyone + 2 * SIDE * rows) * unit,
-            bytes_accessed=26 * 1024 * 1024,
-            transcendentals=everyone * ff,
-        ),
-        name="expert_backward",
-    )(pos, gathered, wg, wu, wd)
-    grads = [pull(pieces[d], "y", SIDE - d) for d in range(SIDE)]
-
     pieces = pl.pallas_call(
         functools.partial(forward_kernel, tokens, width, table_at, experts),
         out_shape=[jax.ShapeDtypeStruct((rows, width), BF16)] * SIDE,
@@ -321,19 +309,56 @@
             pltpu.VMEM((SIDE * rows, width), BF16),
         ]
         + weight_scratch
-        + [pltpu.SemaphoreType.DMA((SIDE,)), pltpu.SemaphoreType.DMA((3,))],
+        + [pltpu.SemaphoreType.DMA((SIDE * SIDE,)), pltpu.SemaphoreType.DMA((3,))],
         compiler_params=params,
         cost_estimate=pl.CostEstimate(
             flops=3 * SIDE * rows * unit, bytes_accessed=18 * 1024 * 1024, transcendentals=SIDE * rows * ff
         ),
         name="expert_forward",
     )(pos, gathered, wg, wu, wd)
-    outs = [pull(pieces[d], "z", SIDE - d) for d in range(SIDE)]
-
-    def combine(parts, along, lane, weighted):
+    outs = [pull(pieces[d], "y", SIDE - d) for d in range(SIDE)]
+
+    after, _ = lax.optimization_barrier((pos, pieces))
+    steps = 2
+    group, slots = everyone // steps, experts * CAP // steps
+    wide = width + LANES
+
+    def slot_spec(columns):
+        return pl.BlockSpec((slots, columns), lambda i: (i, 0))
+
+    *pieces, d_gate, d_up, gated, packed = pl.pallas_call(
+        functools.partial(backward_kernel, tokens, width),
+        grid=(steps,),
+        out_shape=[jax.ShapeDtypeStruct((rows, wide), BF16)] * SIDE
+        + [jax.ShapeDtypeStruct((experts * CAP, ff), BF16)] * 3
+        + [jax.ShapeDtypeStruct((experts * CAP, 2 * width), BF16)],
+        in_specs=[
+            SMEM,
+            pl.BlockSpec((group, 2 * width), lambda i: (i, 0)),
+            pl.BlockSpec((group, LANES), lambda i: (i, table_at // LANES)),
+        ]
+        + [ANY] * 3,
+        out_specs=[ANY] * SIDE + [slot_spec(ff)] * 3 + [slot_spec(2 * width)],
+        scratch_shapes=[pltpu.VMEM((experts * CAP, wide), BF16)]
+        + weight_scratch
+        + [
+            pltpu.SemaphoreType.DMA((3,)),
+            pltpu.SemaphoreType.DMA((SIDE,)),
+        ],
+        compiler_params=params,
+        cost_estimate=pl.CostEstimate(
+            flops=5 * SIDE * rows * unit, bytes_accessed=26 * 1024 * 1024, transcendentals=SIDE * rows * ff
+        ),
+        name="expert_backward",
+    )(after, gathered, gathered, wg, wu, wd)
+    grads = [pull(pieces[d], "z", SIDE - d) for d in range(SIDE)]
+
+    tables = gathered[:, table_at : table_at + LANES]
+
+    def combine(at, parts, along, lane, weighted):
         wide = parts[0].shape[1]
         return pl.pallas_call(
-            functools.partial(combine_kernel, tokens, along, table_at, lane, weighted),
+            functools.partial(combine_kernel, tokens, along, 0, lane, weighted),
             out_shape=[jax.ShapeDtypeStruct((tokens, wide), BF16)] * SIDE,
             in_specs=[SMEM, ANY] + [VMEM] * SIDE,
             out_specs=[VMEM] * SIDE,
@@ -343,17 +368,20 @@
                 flops=2 * SIDE * tokens * rows * wide, bytes_accessed=5 * 1024 * 1024, transcendentals=0
             ),
             name="combine_" + along,
-        )(pos, gathered, *parts)
-
-    partial = combine(grads, "y", 0, False)
-    summed = sum(pull(partial[d], "z", SIDE - d).astype(F32) for d in range(SIDE))
-    partial = combine(outs, "z", experts, True)
-    mixed = sum(pull(partial[d], "y", SIDE - d).astype(F32) for d in range(SIDE))
+        )(at, tables, *parts)
+
+    grad_gate = mm(packed[:, :width], d_gate, TN).astype(BF16)
+    grad_up = mm(packed[:, :width], d_up, TN).astype(BF16)
+
+    partial = combine(pos, outs, "y", experts, True)
+    mixed = sum(pull(partial[d], "z", SIDE - d).astype(F32) for d in range(SIDE))
     fwd_out = (arrived.astype(F32) + mixed).astype(BF16)
 
-    grad_gate = mm(gathered[:, :width], d_gate, TN).astype(BF16)
-    grad_up = mm(gathered[:, :width], d_up, TN).astype(BF16)
-    grad_down = mm(gated, gathered[:, width : 2 * width], TN).astype(BF16)
+    later, grad_gate, grad_up = lax.optimization_barrier((pos, grad_gate, grad_up))
+    partial = combine(later, grads, "z", 0, False)
+    gated, partial = lax.optimization_barrier((gated, partial))
+    summed = sum(pull(partial[d], "y", SIDE - d).astype(F32) for d in range(SIDE))
+    grad_down = mm(gated, packed[:, width:], TN).astype(BF16)
 
     gate_grad = jnp.sum(hit_prev * summed[:, None, width : width + experts], axis=2).astype(BF16)
     dxhat = summed[:, :width] * gain

time: 230 us -> 228 us (level)
  Pallas kernels: 50.3 us -> 44.1 us
  waiting for transfers between devices: 113 us -> 119 us
  matrix products: 21.9 us -> 16.3 us
  starting transfers between devices: 19.7 us -> 22.8 us
    pallas_call x3, Pallas kernels: 36.1 us -> 30.4 us  [the longest x1 24.9 us: per_device(): pl.pallas_call(functools.partial(backward_kernel, tokens, width), grid=(s...]
    dot_general x3, matrix products: 21.9 us -> 16.3 us  [mm(): return lax.dot_general(a, b, (dims, ((), ())), preferred_element_type=F32)]
    ppermute x12, waiting for transfers between devices: 20.7 us -> 25.9 us  [pull(): return lax.ppermute(array, 'expert', pairs)]
    ppermute x12, starting transfers between devices: 16.7 us -> 19.8 us  [pull(): return lax.ppermute(array, 'expert', pairs)]
  transfers between devices with their start and end apart: 15 -> 15, of which waited for: 4 -> 3; matrix products, arithmetic and copies ran while one was open for 13% -> 11% of each run, Pallas kernels for 16% -> 13%
where the time goes in v2:
time: 228 us; the launch traced here: 227 us
  waiting for transfers between devices  119 us (52%)
  Pallas kernels  44.1 us (19%)
  starting transfers between devices  22.8 us (10%)
  matrix products  16.3 us (7%)
  between operations  14.2 us (6%)
  other arithmetic  9.79 us (4%)
    all_gather x1, waiting for transfers between devices, per_device(): gathered = lax.all_gather(bundle, 'expert', axis=0, tiled=True)  92.7 us
    ppermute x12, waiting for transfers between devices, pull(): return lax.ppermute(array, 'expert', pairs)  25.9 us
    pallas_call x1, Pallas kernels, per_device(): pl.pallas_call(functools.partial(backward_kernel, tokens, width), grid=(s...  24.9 us
    ppermute x12, starting transfers between devices, pull(): return lax.ppermute(array, 'expert', pairs)  19.8 us
    dot_general x3, matrix products, mm(): return lax.dot_general(a, b, (dims, ((), ())), preferred_element_type=F32)  16.3 us
    pallas_call x1, Pallas kernels, per_device(): pl.pallas_call(functools.partial(forward_kernel, tokens, width, table_at,...  13.7 us
    pallas_call x2, Pallas kernels, combine(): pl.pallas_call(functools.partial(combine_kernel, tokens, along, 0, lane,...  5.41 us
  transfers between devices with their start and end apart: 15, of which 3 were waited for; matrix products, arithmetic and copies ran while one was open for 11% of the time, Pallas kernels for 13%

profile of v2, /device:TPU:0, one launch (start us, length us, event | category | flops | bytes accessed | tf_op | source)
XLA Modules:
  0.0 227.2 jit_solution(9684332963927435173)
XLA Ops:
  7.2 2.9 %collective-permute-start.1 = (bf16[64,2048]{1,0:T(8,128)(2,1)}, bf16[64,2048]{1,0:T(8,128)(2,1)S(1)}, u32[]{:S(2)}, u32[]{:S(2)}) collective-permute-start(bf16[64,2048]{1,0:T(8,128)(2,1)} %bitcast.51), channel_id=1, source_target_pairs={{0,112},{16,0},{32,16},{48,32},{64,48},{80,64},{96,80},{112,96},{1... | collective-permute-start | bytes 786440 | tf_op jit(solution)/shard_map/ppermute | solution.py:25
  10.2 1.1 fusion.15
  11.3 0.7 bitcast_convert_fusion
  12.0 0.7 select_reduce_fusion.1
  12.8 0.7 bitcast_convert_fusion.1
  13.5 0.7 select_reduce_fusion.2
  14.4 0.7 mul.110
  15.3 1.1 fusion.9
  16.4 0.9 pad_maximum_fusion
  17.5 92.7 %all-gather.2.cloned.1.call-done.gathered.both.table = bf16[1024,6272]{1,0:T(8,128)(2,1)} async-done(((bf16[64,6272]{1,0:T(8,128)(2,1)}), bf16[1024,6272]{1,0:T(8,128)(2,1)}) %all-gather.2.cloned.1.call-update) | async-done | bytes 12845072 | tf_op jit(solution)/shard_map/all_gather | solution.py:293
  110.2 13.7 %expert_forward.1 = (bf16[192,2048]{1,0:T(8,128)(2,1)S(1)}, bf16[192,2048]{1,0:T(8,128)(2,1)S(1)}, bf16[192,2048]{1,0:T(8,128)(2,1)S(1)}, bf16[192,2048]{1,0:T(8,128)(2,1)S(1)}) custom-call(s32[3]{0:T(128)S(1)} %pad_add_fusion.pos, bf16[1024,6272]{1,0:T(8,128)(2,1)} %all-gather.2.cloned.1.call-done.gathered.both.table, bf16[2048,768]{1,0:T(8,128)(2,1)} %bitcast.44, ...), custom_call_target="tpu_custom_call" | custom-call | flops 7247757312 | bytes 18874368 | tf_op jit(solution)/shard_map/expert_forward/pallas_call | solution.py:302
  123.9 1.5 collective-permute-start.2
  125.4 2.7 %collective-permute-start.3 = (bf16[192,2048]{1,0:T(8,128)(2,1)S(1)}, bf16[192,2048]{1,0:T(8,128)(2,1)S(1)}, u32[]{:S(2)}, u32[]{:S(2)}) collective-permute-start(bf16[192,2048]{1,0:T(8,128)(2,1)S(1)} %get-tuple-element.37), channel_id=1, source_target_pairs={{2,0},{3,1},{0,2},{1,3},{6,4},{7,5},{4,6},{5,7},{10,8},{11,9},{8,1... | collective-permute-start | bytes 2359304 | tf_op jit(solution)/shard_map/ppermute | solution.py:36
  128.1 1.4 collective-permute-start.4
  129.6 24.9 %expert_backward.1 = (bf16[192,2176]{1,0:T(8,128)(2,1)S(1)}, bf16[192,2176]{1,0:T(8,128)(2,1)S(1)}, bf16[192,2176]{1,0:T(8,128)(2,1)S(1)}, bf16[192,2176]{1,0:T(...) custom-call(s32[3]{0:T(128)S(1)} %pad_add_fusion.pos, ...), custom_call_target="tpu_custom_call" | custom-call | flops 12079595520 | bytes 27262976 | tf_op jit(solution)/shard_map/expert_backward/pallas_call | solution.py:329
  154.5 0.3 collective-permute-start.8
  154.8 2.5 %collective-permute-start.9 = (bf16[192,2176]{1,0:T(8,128)(2,1)S(1)}, bf16[192,2176]{1,0:T(8,128)(2,1)S(1)}, u32[]{:S(2)}, u32[]{:S(2)}) collective-permute-start(bf16[192,2176]{1,0:T(8,128)(2,1)S(1)} %get-tuple-element.51), channel_id=1, source_target_pairs={{8,0},{9,1},{10,2},{11,3},{12,4},{13,5},{14,6},{15,7},{0,8},{1,9},... | collective-permute-start | bytes 2506760 | tf_op jit(solution)/shard_map/ppermute | solution.py:36
  157.3 6.8 %collective-permute-start.10 = (bf16[192,2176]{1,0:T(8,128)(2,1)S(1)}, bf16[192,2176]{1,0:T(8,128)(2,1)S(1)}, u32[]{:S(2)}, u32[]{:S(2)}) collective-permute-start(bf16[192,2176]{1,0:T(8,128)(2,1)S(1)} %get-tuple-element.52), channel_id=1, source_target_pairs={{4,0},{5,1},{6,2},{7,3},{8,4},{9,5},{10,6},{11,7},{12,8},{13,9},{1... | collective-permute-start | bytes 2506760 | tf_op jit(solution)/shard_map/ppermute | solution.py:36
  164.1 6.4 %convolution_convert_fusion.2 = bf16[2048,768]{1,0:T(8,128)(2,1)} fusion(bf16[768,768]{1,0:T(8,128)(2,1)S(1)} %get-tuple-element.46, bf16[768,4096]{1,0:T(8,128)(2,1)} %get-tuple-element.45), kind=kOutput, calls=%fused_computation.2 | convolution fusion | flops 2417491968 | bytes 7471104 | tf_op jit(solution)/shard_map/dot_general | solution.py:40
  170.5 4.0 %convolution_convert_fusion.1 = bf16[2048,768]{1,0:T(8,128)(2,1)} fusion(bf16[768,768]{1,0:T(8,128)(2,1)S(1)} %get-tuple-element.47, bf16[768,4096]{1,0:T(8,128)(2,1)S(1)} %copy-done.2), kind=kOutput, calls=%fused_computation.1 | convolution fusion | flops 2417491968 | bytes 7471104 | tf_op jit(solution)/shard_map/dot_general | solution.py:40
  174.5 1.0 slice.21.gathered
  175.5 2.6 %combine_y.1 = (bf16[64,2048]{1,0:T(8,128)(2,1)S(1)}, bf16[64,2048]{1,0:T(8,128)(2,1)S(1)}, bf16[64,2048]{1,0:T(8,128)(2,1)S(1)}, bf16[64,2048]{1,0:T(8,128)(2,1)S(1)}) custom-call(s32[3]{0:T(128)S(1)} %pad_add_fusion.pos, bf16[1024,128]{1,0:T(8,128)(2,1)S(1)} %slice.21.gathered, bf16[192,2048]{1,0:T(8,128)(2,1)S(1)} %get-tuple-element.35.rest_0_, ...), custom_call_target="tpu_custom_call" | custom-call | flops 201326592 | bytes 5242880 | tf_op jit(solution)/shard_map/combine_y/pallas_call | solution.py:360
  178.1 0.8 collective-permute-start.7
  179.0 19.1 %collective-permute-done.8.rest_1_ = bf16[192,2176]{1,0:T(8,128)(2,1)S(1)} collective-permute-done((bf16[192,2176]{1,0:T(8,128)(2,1)S(1)}, bf16[192,2176]{1,0:T(8,128)(2,1)S(1)}, u32[]{:S(2)}, u32[]{:S(2)}) %collective-permute-start.8) | collective-permute-done | bytes 835616 | tf_op jit(solution)/shard_map/ppermute | solution.py:36
  198.1 2.8 %combine_z.1 = (bf16[64,2176]{1,0:T(8,128)(2,1)S(1)}, bf16[64,2176]{1,0:T(8,128)(2,1)S(1)}, bf16[64,2176]{1,0:T(8,128)(2,1)S(1)}, bf16[64,2176]{1,0:T(8,128)(2,1)S(1)}) custom-call(s32[3]{0:T(128)S(1)} %pad_add_fusion.pos, bf16[1024,128]{1,0:T(8,128)(2,1)S(1)} %slice.21.gathered, bf16[192,2176]{1,0:T(8,128)(2,1)S(1)} %get-tuple-element.49.rest_0_, ...), custom_call_target="tpu_custom_call" | custom-call | flops 213909504 | bytes 5242880 | tf_op jit(solution)/shard_map/combine_z/pallas_call | solution.py:360
  200.8 0.2 collective-permute-start.13
  201.1 3.5 %collective-permute-start.12 = (bf16[64,2176]{1,0:T(8,128)(2,1)S(1)}, bf16[64,2176]{1,0:T(8,128)(2,1)S(1)}, u32[]{:S(2)}, u32[]{:S(2)}) collective-permute-start(bf16[64,2176]{1,0:T(8,128)(2,1)S(1)} %get-tuple-element.59), channel_id=1, source_target_pairs={{2,0},{3,1},{0,2},{1,3},{6,4},{7,5},{4,6},{5,7},{10,8},{11,9},{8,1... | collective-permute-start | bytes 835592 | tf_op jit(solution)/shard_map/ppermute | solution.py:36
  204.6 5.9 %fusion.1 = bf16[1,1,768,2048]{3,2,1,0:T(8,128)(2,1)} fusion(bf16[768,768]{1,0:T(8,128)(2,1)S(1)} %copy-done.3, bf16[768,4096]{1,0:T(8,128)(2,1)} %get-tuple-element.45), kind=kOutput, calls=%fused_computation.4 | convolution fusion | flops 2417491968 | bytes 7471104 | tf_op jit(solution)/shard_map/dot_general | solution.py:40
  210.6 0.9 fusion.20
  211.5 6.8 %collective-permute-done.11 = bf16[64,2176]{1,0:T(8,128)(2,1)S(1)} collective-permute-done((bf16[64,2176]{1,0:T(8,128)(2,1)S(1)}, bf16[64,2176]{1,0:T(8,128)(2,1)S(1)}, u32[]{:S(2)}, u32[]{:S(2)}) %collective-permute-start.11) | collective-permute-done | bytes 278560 | tf_op jit(solution)/shard_map/ppermute | solution.py:36
  218.8 0.6 select_reduce_fusion
  219.4 0.9 fusion.21
  (38 shorter events, 1.2 us)
Async XLA Ops:
  7.2 103.0 %all-gather.2.cloned.1.call-start = ((), (), s32[]{:S(2)}) async-start(), calls=%async_computation | async-start | bytes 13647872 | tf_op jit(solution)/shard_map/all_gather | solution.py:293
  7.2 7.9 %collective-permute-start = (bf16[64,2048]{1,0:T(8,128)(2,1)}, bf16[64,2048]{1,0:T(8,128)(2,1)S(1)}, u32[]{:S(2)}, u32[]{:S(2)}) collective-permute-start(bf16[64,2048]{1,0:T(8,128)(2,1)} %bitcast.50), channel_id=1, source_target_pairs={{0,16},{16,32},{32,48},{48,64},{64,80},{80,96},{96,112},{112,0},{1... | collective-permute-start | bytes 786440 | tf_op jit(solution)/shard_map/ppermute | solution.py:25
  7.2 9.2 %collective-permute-start.1 = (bf16[64,2048]{1,0:T(8,128)(2,1)}, bf16[64,2048]{1,0:T(8,128)(2,1)S(1)}, u32[]{:S(2)}, u32[]{:S(2)}) collective-permute-start(bf16[64,2048]{1,0:T(8,128)(2,1)} %bitcast.51), channel_id=1, source_target_pairs={{0,112},{16,0},{32,16},{48,32},{64,48},{80,64},{96,80},{112,96},{1... | collective-permute-start | bytes 786440 | tf_op jit(solution)/shard_map/ppermute | solution.py:25
  123.9 33.4 %collective-permute-start.2 = (bf16[192,2048]{1,0:T(8,128)(2,1)S(1)}, bf16[192,2048]{1,0:T(8,128)(2,1)S(1)}, u32[]{:S(2)}, u32[]{:S(2)}) collective-permute-start(bf16[192,2048]{1,0:T(8,128)(2,1)S(1)} %get-tuple-element.36), channel_id=1, source_target_pairs={{3,0},{0,1},{1,2},{2,3},{7,4},{4,5},{5,6},{6,7},{11,8},{8,9},{9,10... | collective-permute-start | bytes 2359304 | tf_op jit(solution)/shard_map/ppermute | solution.py:36
  125.4 50.1 %collective-permute-start.3 = (bf16[192,2048]{1,0:T(8,128)(2,1)S(1)}, bf16[192,2048]{1,0:T(8,128)(2,1)S(1)}, u32[]{:S(2)}, u32[]{:S(2)}) collective-permute-start(bf16[192,2048]{1,0:T(8,128)(2,1)S(1)} %get-tuple-element.37), channel_id=1, source_target_pairs={{2,0},{3,1},{0,2},{1,3},{6,4},{7,5},{4,6},{5,7},{10,8},{11,9},{8,1... | collective-permute-start | bytes 2359304 | tf_op jit(solution)/shard_map/ppermute | solution.py:36
  128.1 47.3 %collective-permute-start.4 = (bf16[192,2048]{1,0:T(8,128)(2,1)S(1)}, bf16[192,2048]{1,0:T(8,128)(2,1)S(1)}, u32[]{:S(2)}, u32[]{:S(2)}) collective-permute-start(bf16[192,2048]{1,0:T(8,128)(2,1)S(1)} %get-tuple-element.38), channel_id=1, source_target_pairs={{1,0},{2,1},{3,2},{0,3},{5,4},{6,5},{7,6},{4,7},{9,8},{10,9},{11,1... | collective-permute-start | bytes 2359304 | tf_op jit(solution)/shard_map/ppermute | solution.py:36
  154.5 43.5 %collective-permute-start.8 = (bf16[192,2176]{1,0:T(8,128)(2,1)S(1)}, bf16[192,2176]{1,0:T(8,128)(2,1)S(1)}, u32[]{:S(2)}, u32[]{:S(2)}) collective-permute-start(bf16[192,2176]{1,0:T(8,128)(2,1)S(1)} %get-tuple-element.50), channel_id=1, source_target_pairs={{12,0},{13,1},{14,2},{15,3},{0,4},{1,5},{2,6},{3,7},{4,8},{5,9},{6... | collective-permute-start | bytes 2506760 | tf_op jit(solution)/shard_map/ppermute | solution.py:36
  154.8 43.2 %collective-permute-start.9 = (bf16[192,2176]{1,0:T(8,128)(2,1)S(1)}, bf16[192,2176]{1,0:T(8,128)(2,1)S(1)}, u32[]{:S(2)}, u32[]{:S(2)}) collective-permute-start(bf16[192,2176]{1,0:T(8,128)(2,1)S(1)} %get-tuple-element.51), channel_id=1, source_target_pairs={{8,0},{9,1},{10,2},{11,3},{12,4},{13,5},{14,6},{15,7},{0,8},{1,9},... | collective-permute-start | bytes 2506760 | tf_op jit(solution)/shard_map/ppermute | solution.py:36
  157.3 40.8 %collective-permute-start.10 = (bf16[192,2176]{1,0:T(8,128)(2,1)S(1)}, bf16[192,2176]{1,0:T(8,128)(2,1)S(1)}, u32[]{:S(2)}, u32[]{:S(2)}) collective-permute-start(bf16[192,2176]{1,0:T(8,128)(2,1)S(1)} %get-tuple-element.52), channel_id=1, source_target_pairs={{4,0},{5,1},{6,2},{7,3},{8,4},{9,5},{10,6},{11,7},{12,8},{13,9},{1... | collective-permute-start | bytes 2506760 | tf_op jit(solution)/shard_map/ppermute | solution.py:36
  164.1 6.4 %copy-start.2 = (bf16[768,4096]{1,0:T(8,128)(2,1)S(1)}, bf16[768,4096]{1,0:T(8,128)(2,1)}, u32[]{:S(2)}) copy-start(bf16[768,4096]{1,0:T(8,128)(2,1)} %get-tuple-element.45) | copy-start | bytes 18874372
  175.5 29.1 %copy-start.3 = (bf16[768,768]{1,0:T(8,128)(2,1)S(1)}, bf16[768,768]{1,0:T(8,128)(2,1)}, u32[]{:S(2)}) copy-start(bf16[768,768]{1,0:T(8,128)(2,1)} %get-tuple-element.63) | copy-start | bytes 3538948
  178.1 32.3 %collective-permute-start.7 = (bf16[64,2048]{1,0:T(8,128)(2,1)S(1)}, bf16[64,2048]{1,0:T(8,128)(2,1)S(1)}, u32[]{:S(2)}, u32[]{:S(2)}) collective-permute-start(bf16[64,2048]{1,0:T(8,128)(2,1)S(1)} %get-tuple-element.42), channel_id=1, source_target_pairs={{4,0},{5,1},{6,2},{7,3},{8,4},{9,5},{10,6},{11,7},{12,8},{13,9},{1... | collective-permute-start | bytes 786440 | tf_op jit(solution)/shard_map/ppermute | solution.py:36
  179.0 31.6 %collective-permute-start.6 = (bf16[64,2048]{1,0:T(8,128)(2,1)S(1)}, bf16[64,2048]{1,0:T(8,128)(2,1)S(1)}, u32[]{:S(2)}, u32[]{:S(2)}) collective-permute-start(bf16[64,2048]{1,0:T(8,128)(2,1)S(1)} %get-tuple-element.41), channel_id=1, source_target_pairs={{8,0},{9,1},{10,2},{11,3},{12,4},{13,5},{14,6},{15,7},{0,8},{1,9},... | collective-permute-start | bytes 786440 | tf_op jit(solution)/shard_map/ppermute | solution.py:36
  198.0 12.5 %collective-permute-start.5 = (bf16[64,2048]{1,0:T(8,128)(2,1)S(1)}, bf16[64,2048]{1,0:T(8,128)(2,1)S(1)}, u32[]{:S(2)}, u32[]{:S(2)}) collective-permute-start(bf16[64,2048]{1,0:T(8,128)(2,1)S(1)} %get-tuple-element.40), channel_id=1, source_target_pairs={{12,0},{13,1},{14,2},{15,3},{0,4},{1,5},{2,6},{3,7},{4,8},{5,9},{6... | collective-permute-start | bytes 786440 | tf_op jit(solution)/shard_map/ppermute | solution.py:36
  200.8 10.6 %collective-permute-start.13 = (bf16[64,2176]{1,0:T(8,128)(2,1)S(1)}, bf16[64,2176]{1,0:T(8,128)(2,1)S(1)}, u32[]{:S(2)}, u32[]{:S(2)}) collective-permute-start(bf16[64,2176]{1,0:T(8,128)(2,1)S(1)} %get-tuple-element.60), channel_id=1, source_target_pairs={{1,0},{2,1},{3,2},{0,3},{5,4},{6,5},{7,6},{4,7},{9,8},{10,9},{11,1... | collective-permute-start | bytes 835592 | tf_op jit(solution)/shard_map/ppermute | solution.py:36
  201.1 10.4 %collective-permute-start.12 = (bf16[64,2176]{1,0:T(8,128)(2,1)S(1)}, bf16[64,2176]{1,0:T(8,128)(2,1)S(1)}, u32[]{:S(2)}, u32[]{:S(2)}) collective-permute-start(bf16[64,2176]{1,0:T(8,128)(2,1)S(1)} %get-tuple-element.59), channel_id=1, source_target_pairs={{2,0},{3,1},{0,2},{1,3},{6,4},{7,5},{4,6},{5,7},{10,8},{11,9},{8,1... | collective-permute-start | bytes 835592 | tf_op jit(solution)/shard_map/ppermute | solution.py:36
  210.5 8.0 %copy-start = (bf16[1,64,2048]{2,1,0:T(8,128)(2,1)S(1)}, bf16[1,64,2048]{2,1,0:T(8,128)(2,1)}, u32[]{:S(2)}) copy-start(bf16[1,64,2048]{2,1,0:T(8,128)(2,1)} %param.12) | copy-start | bytes 786436
  210.5 8.3 %copy-start.1 = (s32[1,64,8]{1,2,0:T(8,128)S(1)}, s32[1,64,8]{1,2,0:T(8,128)}, u32[]{:S(2)}) copy-start(s32[1,64,8]{1,2,0:T(8,128)} %param.20) | copy-start | bytes 6148
  210.5 7.8 %collective-permute-start.11 = (bf16[64,2176]{1,0:T(8,128)(2,1)S(1)}, bf16[64,2176]{1,0:T(8,128)(2,1)S(1)}, u32[]{:S(2)}, u32[]{:S(2)}) collective-permute-start(bf16[64,2176]{1,0:T(8,128)(2,1)S(1)} %get-tuple-element.58), channel_id=1, source_target_pairs={{3,0},{0,1},{1,2},{2,3},{7,4},{4,5},{5,6},{6,7},{11,8},{8,9},{9,10... | collective-permute-start | bytes 835592 | tf_op jit(solution)/shard_map/ppermute | solution.py:36
Sparse Core Ops, SparseCore 0:
  17.5 92.6 all-gather.1

commit v3 on v2

--- a/solution.py
+++ b/solution.py
@@ -158,15 +158,14 @@
 
 
 def forward_kernel(tokens, width, offset, lane, pos, gathered, wg, wu, wd, *rest):
-    pieces = rest[:SIDE]
-    held, packed, wg_v, wu_v, wd_v, sems, weight_sems = rest[SIDE:]
-    me, y = pos[0], pos[2]
+    out, held, packed, wg_v, wu_v, wd_v, sems, weight_sems = rest
+    me = pos[0]
     group = SIDE * tokens
     rows = SIDE * CAP
     wide = held.shape[1]
 
     def block_copy(d, zb):
-        start = pl.multiple_of((zb * SIDE + lax.rem(y + d, SIDE)) * tokens, tokens)
+        start = pl.multiple_of((zb * SIDE + d) * tokens, tokens)
         return pltpu.make_async_copy(
             gathered.at[pl.ds(start, tokens), pl.ds(offset, wide)],
             held.at[pl.ds(pl.multiple_of(d * group + zb * tokens, tokens), tokens), :],
@@ -201,21 +200,17 @@
         pre_gate = mm(packed[at, :], wg_v[...])
         pre_up = mm(packed[at, :], wu_v[...])
         hidden = (pre_gate * jax.nn.sigmoid(pre_gate) * pre_up).astype(BF16)
-        out = mm(hidden, wd_v[...]).astype(BF16)
-        for k in range(SIDE // 2):
-
-            @pl.when(c == k)
-            def _():
-                pieces[2 * k][...] = out[:rows]
-                pieces[2 * k + 1][...] = out[rows:]
-
+        out[at, :] = mm(hidden, wd_v[...]).astype(BF16)
         return carry
 
     lax.fori_loop(0, SIDE // 2, tile, 0)
 
 
-def combine_kernel(tokens, along, offset, lane, weighted, pos, gathered, *rest):
-    rows, outs, (tables, sems) = rest[:SIDE], rest[SIDE : 2 * SIDE], rest[2 * SIDE :]
+def combine_kernel(tokens, along, offset, lane, weighted, whole, pos, gathered, *rest):
+    parts = 1 if whole else SIDE
+    rows, outs, (tables, sems) = rest[:parts], rest[parts : 2 * parts], rest[2 * parts :]
+    if whole:
+        rows = [rest[0].at[pl.ds(j * SIDE * CAP, SIDE * CAP), :] for j in range(SIDE)]
     z, y = pos[1], pos[2]
 
     def block_of(d):
@@ -236,7 +231,7 @@
     owner = jnp.zeros((LANES, SIDE * CAP), jnp.int32)
     for j in range(SIDE):
         if along == "y":
-            expert = z * SIDE + lax.rem(y + SIDE - j, SIDE)
+            expert = z * SIDE + (j if whole else lax.rem(y + SIDE - j, SIDE))
         else:
             expert = lax.rem(z + SIDE - j, SIDE) * SIDE + y
         owner = jnp.where(column // CAP == j, expert + lane, owner)
@@ -250,7 +245,10 @@
         matrix = jnp.where(here, value, 0.0).astype(BF16)
         at = pl.ds(pl.multiple_of(block_of(d) * CAP, CAP), CAP)
         mine = jnp.concatenate([part[at, :] for part in rows], axis=0)
-        outs[d][...] = mm(matrix, mine).astype(BF16)
+        if whole:
+            outs[0][pl.ds(pl.multiple_of(block_of(d) * tokens, tokens), tokens), :] = mm(matrix, mine).astype(BF16)
+        else:
+            outs[d][...] = mm(matrix, mine).astype(BF16)
 
 
 ANY = pl.BlockSpec(memory_space=pl.ANY)
@@ -299,11 +297,11 @@
         pltpu.VMEM(wd.shape, BF16),
     ]
     unit = 2 * width * ff
-    pieces = pl.pallas_call(
+    out = pl.pallas_call(
         functools.partial(forward_kernel, tokens, width, table_at, experts),
-        out_shape=[jax.ShapeDtypeStruct((rows, width), BF16)] * SIDE,
+        out_shape=jax.ShapeDtypeStruct((SIDE * rows, width), BF16),
         in_specs=[SMEM] + [ANY] * 4,
-        out_specs=[VMEM] * SIDE,
+        out_specs=VMEM,
         scratch_shapes=[
             pltpu.VMEM((everyone, width + LANES), BF16),
             pltpu.VMEM((SIDE * rows, width), BF16),
@@ -316,9 +314,12 @@
         ),
         name="expert_forward",
     )(pos, gathered, wg, wu, wd)
-    outs = [pull(pieces[d], "y", SIDE - d) for d in range(SIDE)]
-
-    after, _ = lax.optimization_barrier((pos, pieces))
+    after, out = lax.optimization_barrier((pos, out))
+    lines = [[z * SIDE + y for y in range(SIDE)] for z in range(SIDE)]
+    outs = lax.all_to_all(
+        out.reshape(SIDE, rows, width), "expert", split_axis=0, concat_axis=0, tiled=True, axis_index_groups=lines
+    ).reshape(out.shape)
+
     steps = 2
     group, slots = everyone // steps, experts * CAP // steps
     wide = width + LANES
@@ -358,10 +359,10 @@
     def combine(at, parts, along, lane, weighted):
         wide = parts[0].shape[1]
         return pl.pallas_call(
-            functools.partial(combine_kernel, tokens, along, 0, lane, weighted),
-            out_shape=[jax.ShapeDtypeStruct((tokens, wide), BF16)] * SIDE,
-            in_specs=[SMEM, ANY] + [VMEM] * SIDE,
-            out_specs=[VMEM] * SIDE,
+            functools.partial(combine_kernel, tokens, along, 0, lane, weighted, len(parts) == 1),
+            out_shape=[jax.ShapeDtypeStruct((SIDE * tokens // len(parts), wide), BF16)] * len(parts),
+            in_specs=[SMEM, ANY] + [VMEM] * len(parts),
+            out_specs=[VMEM] * len(parts),
             scratch_shapes=[pltpu.VMEM((SIDE, tokens, LANES), BF16), pltpu.SemaphoreType.DMA((SIDE,))],
             compiler_params=params,
             cost_estimate=pl.CostEstimate(
@@ -370,18 +371,21 @@
             name="combine_" + along,
         )(at, tables, *parts)
 
+    partial = combine(pos, [outs], "y", experts, True)
+    summands = partial[0]
+    across = [[z * SIDE + y for z in range(SIDE)] for y in range(SIDE)]
+    partial = lax.all_to_all(
+        partial[0].reshape(SIDE, tokens, width), "expert", split_axis=0, concat_axis=0, tiled=True, axis_index_groups=across
+    )
+    mixed = jnp.sum(partial.astype(F32), axis=0)
+    fwd_out = (arrived.astype(F32) + mixed).astype(BF16)
+
     grad_gate = mm(packed[:, :width], d_gate, TN).astype(BF16)
     grad_up = mm(packed[:, :width], d_up, TN).astype(BF16)
-
-    partial = combine(pos, outs, "y", experts, True)
-    mixed = sum(pull(partial[d], "z", SIDE - d).astype(F32) for d in range(SIDE))
-    fwd_out = (arrived.astype(F32) + mixed).astype(BF16)
-
-    later, grad_gate, grad_up = lax.optimization_barrier((pos, grad_gate, grad_up))
+    grad_down = mm(gated, packed[:, width:], TN).astype(BF16)
+    later, _ = lax.optimization_barrier((pos, (grad_gate, grad_up, grad_down, summands)))
     partial = combine(later, grads, "z", 0, False)
-    gated, partial = lax.optimization_barrier((gated, partial))
     summed = sum(pull(partial[d], "y", SIDE - d).astype(F32) for d in range(SIDE))
-    grad_down = mm(gated, packed[:, width:], TN).astype(BF16)
 
     gate_grad = jnp.sum(hit_prev * summed[:, None, width : width + experts], axis=2).astype(BF16)
     dxhat = summed[:, :width] * gain

time: 228 us -> 232 us (1.018)
  Pallas kernels: 44.1 us -> 46.6 us
    ppermute x12 -> x6, starting transfers between devices: 19.8 us -> 10.8 us  [pull(): return lax.ppermute(array, 'expert', pairs)]
    all_to_all x0 -> x2, starting transfers between devices: none -> 8.14 us  [the longest x1 4.24 us: per_device(): lax.all_to_all(out.reshape(SIDE, rows, width), 'expert', split_axis=0, co...]
    all_to_all x0 -> x2, waiting for transfers between devices: none -> 5.4 us  [the longest x1 5.39 us: per_device(): lax.all_to_all(partial[0].reshape(SIDE, tokens, width), 'expert', split_a...]
    ppermute x12 -> x6, waiting for transfers between devices: 25.9 us -> 22.4 us  [pull(): return lax.ppermute(array, 'expert', pairs)]
  transfers between devices with their start and end apart: 15 -> 11, of which waited for: 3 -> 5; matrix products, arithmetic and copies ran while one was open for 11% -> 11% of each run, Pallas kernels for 13% -> 13%
where the time goes in v3:
time: 232 us
  waiting for transfers between devices  120 us (52%)
  Pallas kernels  46.6 us (20%)
  starting transfers between devices  21.9 us (9%)
  matrix products  14.4 us (6%)
  between operations  14.3 us (6%)
  other arithmetic  10.8 us (5%)
  local copies, waits for them, and re-layouts  3.01 us (1%)
    all_gather x1, waiting for transfers between devices, per_device(): gathered = lax.all_gather(bundle, 'expert', axis=0, tiled=True)  92.7 us
    pallas_call x1, Pallas kernels, per_device(): pl.pallas_call(functools.partial(backward_kernel, tokens, width), grid=(s...  25.7 us
    ppermute x6, waiting for transfers between devices, pull(): return lax.ppermute(array, 'expert', pairs)  22.4 us
    dot_general x3, matrix products, mm(): return lax.dot_general(a, b, (dims, ((), ())), preferred_element_type=F32)  14.4 us
    pallas_call x1, Pallas kernels, per_device(): pl.pallas_call(functools.partial(forward_kernel, tokens, width, table_at,...  13.4 us
    ppermute x6, starting transfers between devices, pull(): return lax.ppermute(array, 'expert', pairs)  10.8 us
    pallas_call x2, Pallas kernels, combine(): pl.pallas_call(functools.partial(combine_kernel, tokens, along, 0, lane,...  7.53 us
    all_to_all x1, waiting for transfers between devices, per_device(): lax.all_to_all(partial[0].reshape(SIDE, tokens, width), 'expert', split_a...  5.39 us
  transfers between devices with their start and end apart: 11, of which 5 were waited for; matrix products, arithmetic and copies ran while one was open for 11% of the time, Pallas kernels for 13%

profile of v3, /device:TPU:0, one launch (start us, length us, event | category | flops | bytes accessed | tf_op | source)
XLA Modules:
  0.0 231.5 jit_solution(198736830541864289)
XLA Ops:
  7.2 2.9 %collective-permute-start.1 = (bf16[64,2048]{1,0:T(8,128)(2,1)}, bf16[64,2048]{1,0:T(8,128)(2,1)S(1)}, u32[]{:S(2)}, u32[]{:S(2)}) collective-permute-start(bf16[64,2048]{1,0:T(8,128)(2,1)} %bitcast.55), channel_id=1, source_target_pairs={{0,112},{16,0},{32,16},{48,32},{64,48},{80,64},{96,80},{112,96},{1... | collective-permute-start | bytes 786440 | tf_op jit(solution)/shard_map/ppermute | solution.py:25
  10.2 1.1 fusion.12
  11.3 0.7 bitcast_convert_fusion
  12.7 0.7 select_reduce_fusion.2
  13.5 0.7 select_reduce_fusion.1
  14.4 0.7 mul.110
  15.3 1.1 fusion.6
  16.4 1.0 pad_maximum_fusion
  17.5 92.7 %all-gather.2.cloned.1.call-done.gathered.both.table = bf16[1024,6272]{1,0:T(8,128)(2,1)} async-done(((bf16[64,6272]{1,0:T(8,128)(2,1)}), bf16[1024,6272]{1,0:T(8,128)(2,1)}) %all-gather.2.cloned.1.call-update) | async-done | bytes 12845072 | tf_op jit(solution)/shard_map/all_gather | solution.py:291
  110.2 13.4 %expert_forward.1 = bf16[768,2048]{1,0:T(8,128)(2,1)S(1)} custom-call(s32[3]{0:T(128)S(1)} %pad_add_fusion.pos, bf16[1024,6272]{1,0:T(8,128)(2,1)} %all-gather.2.cloned.1.call-done.gathered.both.table, bf16[2048,768]{1,0:T(8,128)(2,1)} %bitcast.48, bf16[2048,768]{1,0:T(8,128)(2,1)} %bitcast.50, bf16[768,2048]{1,0:T(8,128)(2,1)} %bitcast.52), custom_call_target="tpu_custom_call" | custom-call | flops 7247757312 | bytes 18874368 | tf_op jit(solution)/shard_map/expert_forward/pallas_call | solution.py:300
  123.6 1.7 copy-done
  125.4 4.2 %all-to-all-start = ((bf16[4,192,2048]{2,1,0:T(8,128)(2,1)}), bf16[4,192,2048]{2,1,0:T(8,128)(2,1)S(1)}, u32[]{:S(2)}, u32[]{:S(2)}) async-start(bf16[4,192,2048]{2,1,0:T(8,128)(2,1)} %bitcast.40), calls=%async_computation | async-start | bytes 6291456 | tf_op jit(solution)/shard_map/all_to_all | solution.py:319
  129.6 25.7 %expert_backward.1 = (bf16[192,2176]{1,0:T(8,128)(2,1)S(1)}, bf16[192,2176]{1,0:T(8,128)(2,1)}, bf16[192,2176]{1,0:T(8,128)(2,1)}, bf16[192,2176]{1,0:T(8,128)(2...) custom-call(s32[3]{0:T(128)S(1)} %pad_add_fusion.pos, ...), custom_call_target="tpu_custom_call" | custom-call | flops 12079595520 | bytes 27262976 | tf_op jit(solution)/shard_map/expert_backward/pallas_call | solution.py:330
  155.3 0.9 collective-permute-start.2
  156.2 2.6 %collective-permute-start.3 = (bf16[192,2176]{1,0:T(8,128)(2,1)}, bf16[192,2176]{1,0:T(8,128)(2,1)}, u32[]{:S(2)}, u32[]{:S(2)}) collective-permute-start(bf16[192,2176]{1,0:T(8,128)(2,1)} %get-tuple-element.30), channel_id=1, source_target_pairs={{8,0},{9,1},{10,2},{11,3},{12,4},{13,5},{14,6},{15,7},{0,8},{1,9},... | collective-permute-start | bytes 2506760 | tf_op jit(solution)/shard_map/ppermute | solution.py:36
  158.8 1.4 collective-permute-start.4
  160.2 6.4 %convolution_convert_fusion.2 = bf16[2048,768]{1,0:T(8,128)(2,1)} fusion(bf16[768,768]{1,0:T(8,128)(2,1)S(1)} %get-tuple-element.24, bf16[768,4096]{1,0:T(8,128)(2,1)} %get-tuple-element.23), kind=kOutput, calls=%fused_computation.2 | convolution fusion | flops 2417491968 | bytes 7471104 | tf_op jit(solution)/shard_map/dot_general | solution.py:40
  166.5 4.0 %convolution_convert_fusion.1 = bf16[2048,768]{1,0:T(8,128)(2,1)} fusion(bf16[768,768]{1,0:T(8,128)(2,1)S(1)} %get-tuple-element.25, bf16[768,4096]{1,0:T(8,128)(2,1)S(1)} %copy-done.9), kind=kOutput, calls=%fused_computation.1 | convolution fusion | flops 2417491968 | bytes 7471104 | tf_op jit(solution)/shard_map/dot_general | solution.py:40
  170.6 1.0 slice.21.gathered
  171.6 4.0 %convolution_convert_fusion = bf16[768,2048]{1,0:T(8,128)(2,1)} fusion(bf16[768,768]{1,0:T(8,128)(2,1)S(1)} %copy-done.10, bf16[768,4096]{1,0:T(8,128)(2,1)S(1)} %copy-done.9), kind=kOutput, calls=%fused_computation | convolution fusion | flops 2417491968 | bytes 7471104 | tf_op jit(solution)/shard_map/dot_general | solution.py:40
  175.6 3.6 %combine_y.1 = bf16[256,2048]{1,0:T(8,128)(2,1)} custom-call(s32[3]{0:T(128)S(1)} %pad_add_fusion.pos, bf16[1024,128]{1,0:T(8,128)(2,1)S(1)} %slice.21.gathered, bf16[768,2048]{1,0:T(8,128)(2,1)S(1)} %bitcast.39), custom_call_target="tpu_custom_call" | custom-call | flops 201326592 | bytes 5242880 | tf_op jit(solution)/shard_map/combine_y/pallas_call | solution.py:361
  179.2 16.1 %collective-permute-done.3.rest_2_ = bf16[192,2176]{1,0:T(8,128)(2,1)} collective-permute-done((bf16[192,2176]{1,0:T(8,128)(2,1)}, bf16[192,2176]{1,0:T(8,128)(2,1)}, u32[]{:S(2)}, u32[]{:S(2)}) %collective-permute-start.3) | collective-permute-done | bytes 835616 | tf_op jit(solution)/shard_map/ppermute | solution.py:36
  195.5 3.9 %combine_z.1 = (bf16[64,2176]{1,0:T(8,128)(2,1)S(1)}, bf16[64,2176]{1,0:T(8,128)(2,1)S(1)}, bf16[64,2176]{1,0:T(8,128)(2,1)S(1)}, bf16[64,2176]{1,0:T(8,128)(2,1)S(1)}) custom-call(s32[3]{0:T(128)S(1)} %pad_add_fusion.pos, bf16[1024,128]{1,0:T(8,128)(2,1)S(1)} %slice.21.gathered, bf16[192,2176]{1,0:T(8,128)(2,1)S(1)} %copy-done.2, ...), custom_call_target="tpu_custom_call" | custom-call | flops 213909504 | bytes 5242880 | tf_op jit(solution)/shard_map/combine_z/pallas_call | solution.py:361
  199.5 1.8 collective-permute-start.5
  201.3 2.7 %collective-permute-start.6 = (bf16[64,2176]{1,0:T(8,128)(2,1)S(1)}, bf16[64,2176]{1,0:T(8,128)(2,1)S(1)}, u32[]{:S(2)}, u32[]{:S(2)}) collective-permute-start(bf16[64,2176]{1,0:T(8,128)(2,1)S(1)} %get-tuple-element.34), channel_id=1, source_target_pairs={{2,0},{3,1},{0,2},{1,3},{6,4},{7,5},{4,6},{5,7},{10,8},{11,9},{8,1... | collective-permute-start | bytes 835592 | tf_op jit(solution)/shard_map/ppermute | solution.py:36
  203.9 1.5 collective-permute-start.7
  205.4 3.9 %all-to-all-start.1 = ((bf16[4,64,2048]{2,1,0:T(8,128)(2,1)}), bf16[4,64,2048]{2,1,0:T(8,128)(2,1)S(1)}, u32[]{:S(2)}, u32[]{:S(2)}) async-start(bf16[4,64,2048]{2,1,0:T(8,128)(2,1)} %bitcast.17), calls=%async_computation.1 | async-start | bytes 2097152 | tf_op jit(solution)/shard_map/all_to_all | solution.py:377
  209.3 6.1 %collective-permute-done.6 = bf16[64,2176]{1,0:T(8,128)(2,1)S(1)} collective-permute-done((bf16[64,2176]{1,0:T(8,128)(2,1)S(1)}, bf16[64,2176]{1,0:T(8,128)(2,1)S(1)}, u32[]{:S(2)}, u32[]{:S(2)}) %collective-permute-start.6) | collective-permute-done | bytes 278560 | tf_op jit(solution)/shard_map/ppermute | solution.py:36
  215.4 1.1 convert_add_fusion.1
  217.4 0.9 fusion.18
  218.4 5.4 %all-to-all-done.1 = bf16[4,64,2048]{2,1,0:T(8,128)(2,1)S(1)} async-done(((bf16[4,64,2048]{2,1,0:T(8,128)(2,1)}), bf16[4,64,2048]{2,1,0:T(8,128)(2,1)S(1)}, u32[]{:S(2)}, u32[]{:S(2)}) %all-to-all-start.1) | async-done | bytes 1048608 | tf_op jit(solution)/shard_map/all_to_all | solution.py:377
  223.9 0.8 fusion.17
  (45 shorter events, 2.6 us)
Async XLA Ops:
  7.2 103.0 %all-gather.2.cloned.1.call-start = ((), (), s32[]{:S(2)}) async-start(), calls=%async_computation.2 | async-start | bytes 13647872 | tf_op jit(solution)/shard_map/all_gather | solution.py:291
  7.2 7.9 %collective-permute-start = (bf16[64,2048]{1,0:T(8,128)(2,1)}, bf16[64,2048]{1,0:T(8,128)(2,1)S(1)}, u32[]{:S(2)}, u32[]{:S(2)}) collective-permute-start(bf16[64,2048]{1,0:T(8,128)(2,1)} %bitcast.54), channel_id=1, source_target_pairs={{0,16},{16,32},{32,48},{48,64},{64,80},{80,96},{96,112},{112,0},{1... | collective-permute-start | bytes 786440 | tf_op jit(solution)/shard_map/ppermute | solution.py:25
  7.2 9.2 %collective-permute-start.1 = (bf16[64,2048]{1,0:T(8,128)(2,1)}, bf16[64,2048]{1,0:T(8,128)(2,1)S(1)}, u32[]{:S(2)}, u32[]{:S(2)}) collective-permute-start(bf16[64,2048]{1,0:T(8,128)(2,1)} %bitcast.55), channel_id=1, source_target_pairs={{0,112},{16,0},{32,16},{48,32},{64,48},{80,64},{96,80},{112,96},{1... | collective-permute-start | bytes 786440 | tf_op jit(solution)/shard_map/ppermute | solution.py:25
  15.1 108.5 %copy-start.4 = (bf16[64,2048]{1,0:T(8,128)(2,1)}, bf16[64,2048]{1,0:T(8,128)(2,1)S(1)}, u32[]{:S(2)}) copy-start(bf16[64,2048]{1,0:T(8,128)(2,1)S(1)} %collective-permute-done) | copy-start | bytes 786436
  16.4 107.2 %copy-start.6 = (bf16[64,2048]{1,0:T(8,128)(2,1)}, bf16[64,2048]{1,0:T(8,128)(2,1)S(1)}, u32[]{:S(2)}) copy-start(bf16[64,2048]{1,0:T(8,128)(2,1)S(1)} %collective-permute-done.1) | copy-start | bytes 786436
  123.6 1.7 copy-start
  125.4 50.2 %all-to-all-start = ((bf16[4,192,2048]{2,1,0:T(8,128)(2,1)}), bf16[4,192,2048]{2,1,0:T(8,128)(2,1)S(1)}, u32[]{:S(2)}, u32[]{:S(2)}) async-start(bf16[4,192,2048]{2,1,0:T(8,128)(2,1)} %bitcast.40), calls=%async_computation | async-start | bytes 6291456 | tf_op jit(solution)/shard_map/all_to_all | solution.py:319
  155.3 11.2 %copy-start.1 = (bf16[192,2176]{1,0:T(8,128)(2,1)}, bf16[192,2176]{1,0:T(8,128)(2,1)S(1)}, u32[]{:S(2)}) copy-start(bf16[192,2176]{1,0:T(8,128)(2,1)S(1)} %get-tuple-element.28.rest_0_) | copy-start | bytes 2506756
  155.3 23.9 %collective-permute-start.2 = (bf16[192,2176]{1,0:T(8,128)(2,1)}, bf16[192,2176]{1,0:T(8,128)(2,1)}, u32[]{:S(2)}, u32[]{:S(2)}) collective-permute-start(bf16[192,2176]{1,0:T(8,128)(2,1)} %get-tuple-element.29), channel_id=1, source_target_pairs={{12,0},{13,1},{14,2},{15,3},{0,4},{1,5},{2,6},{3,7},{4,8},{5,9},{6... | collective-permute-start | bytes 2506760 | tf_op jit(solution)/shard_map/ppermute | solution.py:36
  156.2 39.1 %collective-permute-start.3 = (bf16[192,2176]{1,0:T(8,128)(2,1)}, bf16[192,2176]{1,0:T(8,128)(2,1)}, u32[]{:S(2)}, u32[]{:S(2)}) collective-permute-start(bf16[192,2176]{1,0:T(8,128)(2,1)} %get-tuple-element.30), channel_id=1, source_target_pairs={{8,0},{9,1},{10,2},{11,3},{12,4},{13,5},{14,6},{15,7},{0,8},{1,9},... | collective-permute-start | bytes 2506760 | tf_op jit(solution)/shard_map/ppermute | solution.py:36
  158.8 36.7 %collective-permute-start.4 = (bf16[192,2176]{1,0:T(8,128)(2,1)}, bf16[192,2176]{1,0:T(8,128)(2,1)}, u32[]{:S(2)}, u32[]{:S(2)}) collective-permute-start(bf16[192,2176]{1,0:T(8,128)(2,1)} %get-tuple-element.31), channel_id=1, source_target_pairs={{4,0},{5,1},{6,2},{7,3},{8,4},{9,5},{10,6},{11,7},{12,8},{13,9},{1... | collective-permute-start | bytes 2506760 | tf_op jit(solution)/shard_map/ppermute | solution.py:36
  160.2 6.4 %copy-start.9 = (bf16[768,4096]{1,0:T(8,128)(2,1)S(1)}, bf16[768,4096]{1,0:T(8,128)(2,1)}, u32[]{:S(2)}) copy-start(bf16[768,4096]{1,0:T(8,128)(2,1)} %get-tuple-element.23) | copy-start | bytes 18874372
  166.5 5.0 %copy-start.10 = (bf16[768,768]{1,0:T(8,128)(2,1)S(1)}, bf16[768,768]{1,0:T(8,128)(2,1)}, u32[]{:S(2)}) copy-start(bf16[768,768]{1,0:T(8,128)(2,1)} %get-tuple-element.26) | copy-start | bytes 3538948
  175.6 19.9 %copy-start.2 = (bf16[192,2176]{1,0:T(8,128)(2,1)S(1)}, bf16[192,2176]{1,0:T(8,128)(2,1)}, u32[]{:S(2)}) copy-start(bf16[192,2176]{1,0:T(8,128)(2,1)} %copy-done.1) | copy-start | bytes 2506756
  195.5 21.0 %copy-start.3 = (bf16[1,64,2048]{2,1,0:T(8,128)(2,1)S(1)}, bf16[1,64,2048]{2,1,0:T(8,128)(2,1)}, u32[]{:S(2)}) copy-start(bf16[1,64,2048]{2,1,0:T(8,128)(2,1)} %param.12) | copy-start | bytes 786436
  199.4 17.4 %copy-start.8 = (s32[1,64,8]{1,2,0:T(8,128)S(1)}, s32[1,64,8]{1,2,0:T(8,128)}, u32[]{:S(2)}) copy-start(s32[1,64,8]{1,2,0:T(8,128)} %param.20) | copy-start | bytes 6148
  199.5 18.0 %copy-start.7 = (bf16[64,2048]{1,0:T(8,128)(2,1)S(1)}, bf16[64,2048]{1,0:T(8,128)(2,1)}, u32[]{:S(2)}) copy-start(bf16[64,2048]{1,0:T(8,128)(2,1)} %copy-done.6) | copy-start | bytes 786436
  199.5 9.9 %collective-permute-start.5 = (bf16[64,2176]{1,0:T(8,128)(2,1)S(1)}, bf16[64,2176]{1,0:T(8,128)(2,1)S(1)}, u32[]{:S(2)}, u32[]{:S(2)}) collective-permute-start(bf16[64,2176]{1,0:T(8,128)(2,1)S(1)} %get-tuple-element.33), channel_id=1, source_target_pairs={{3,0},{0,1},{1,2},{2,3},{7,4},{4,5},{5,6},{6,7},{11,8},{8,9},{9,10... | collective-permute-start | bytes 835592 | tf_op jit(solution)/shard_map/ppermute | solution.py:36
  201.3 14.1 %collective-permute-start.6 = (bf16[64,2176]{1,0:T(8,128)(2,1)S(1)}, bf16[64,2176]{1,0:T(8,128)(2,1)S(1)}, u32[]{:S(2)}, u32[]{:S(2)}) collective-permute-start(bf16[64,2176]{1,0:T(8,128)(2,1)S(1)} %get-tuple-element.34), channel_id=1, source_target_pairs={{2,0},{3,1},{0,2},{1,3},{6,4},{7,5},{4,6},{5,7},{10,8},{11,9},{8,1... | collective-permute-start | bytes 835592 | tf_op jit(solution)/shard_map/ppermute | solution.py:36
  203.9 11.5 %collective-permute-start.7 = (bf16[64,2176]{1,0:T(8,128)(2,1)S(1)}, bf16[64,2176]{1,0:T(8,128)(2,1)}, u32[]{:S(2)}, u32[]{:S(2)}) collective-permute-start(bf16[64,2176]{1,0:T(8,128)(2,1)S(1)} %get-tuple-element.35), channel_id=1, source_target_pairs={{1,0},{2,1},{3,2},{0,3},{5,4},{6,5},{7,6},{4,7},{9,8},{10,9},{11,1... | collective-permute-start | bytes 835592 | tf_op jit(solution)/shard_map/ppermute | solution.py:36
  205.4 18.3 %all-to-all-start.1 = ((bf16[4,64,2048]{2,1,0:T(8,128)(2,1)}), bf16[4,64,2048]{2,1,0:T(8,128)(2,1)S(1)}, u32[]{:S(2)}, u32[]{:S(2)}) async-start(bf16[4,64,2048]{2,1,0:T(8,128)(2,1)} %bitcast.17), calls=%async_computation.1 | async-start | bytes 2097152 | tf_op jit(solution)/shard_map/all_to_all | solution.py:377
  209.3 14.6 %copy-start.5 = (bf16[64,2048]{1,0:T(8,128)(2,1)S(1)}, bf16[64,2048]{1,0:T(8,128)(2,1)}, u32[]{:S(2)}) copy-start(bf16[64,2048]{1,0:T(8,128)(2,1)} %copy-done.4) | copy-start | bytes 786436
Sparse Core Ops, SparseCore 0:
  17.6 92.6 all-gather.1
